TPU v7x, 512 devices: a whole 4x4x16 slice. The times are simulated.
512 devices in a mesh: gx: 8 (over y, z_hi), gy: 16 (over z_lo, core), sa: 4 (over x).
Axes of the slice: x: 4, y: 4, z: 16 (z_hi: 2, z_lo: 8; z = z_hi * 8 + z_lo), core: 2. Of those that a mesh axis runs over, the one named last changes fastest.
Arguments:
- source: bfloat16 [8, 16, 32, 768], P('gx', 'gy', 'sa'), may hold values from -6 to 6
- group_gain: float32 [4], replicated, may hold values from 0.25 to 4
- shot_group: int32 [32], P('sa'), may hold values from 0 to 3
- block_cols: int32 [8, 16, 32, 4], P('gx', 'gy'), may hold values from 0 to 29, as said below
- block_vals: bfloat16 [8, 16, 32, 4, 128, 128], P('gx', 'gy', 'sa')
Outputs:
- east_out: bfloat16 [8, 16, 32, 1536], P('gx', 'gy', 'sa')
- north_out: bfloat16 [8, 16, 32, 1536], P('gx', 'gy', 'sa')
- interior: bfloat16 [8, 16, 32, 1024], P('gx', 'gy', 'sa')
Inputs may be any that keep to these rules, and one draw needn't show every extreme that they name: `block_cols`: in each block row, entry 0 names a west block (6 to 17), entry 1 a south block (18 to 29), the other entries distinct source blocks (below 6).
All inputs are finite; a program needn't handle non-finite values.
Results may differ from a plain program's by a relative error of at most 0.02.
Values may be sent and summed in bfloat16 or wider, within the bound.
A program may use at most 64 MiB of HBM per device.

v0:
```python
import jax
import jax.numpy as jnp
from jax import lax
from jax.sharding import PartitionSpec as P

NT = 12


def from_behind(block, axis, distance):
    devices = range(lax.axis_size(axis))
    route = [(i - distance, i) for i in devices if i - distance in devices]
    return lax.ppermute(block, axis, route)


def apply_blocks(inputs, columns, values, width):
    stacked = inputs.reshape(inputs.shape[0], -1, width)
    picked = jnp.take(stacked, columns, axis=1)
    return jnp.einsum("nokc,okcd->nod", picked, values, preferred_element_type=jnp.float32)


def on_device(source, group_gain, shot_group, block_cols, block_vals):
    columns = block_cols[0, 0]
    own_values = block_vals[0, 0]
    width = own_values.shape[-1]
    own_count = own_values.shape[0]
    values = lax.all_gather(block_vals, "sa", axis=2, tiled=True)[0, 0]
    rows = source.shape[2]
    groups = group_gain.shape[0]
    selector = (shot_group[:, None] == jnp.arange(groups, dtype=jnp.int32)[None, :]).astype(
        jnp.float32
    )
    gains = jnp.dot(selector, group_gain, precision=lax.Precision.HIGHEST)
    scaled = (source[0, 0].astype(jnp.float32) * gains[:, None]).astype(jnp.bfloat16)
    block_count = 1
    piece = rows // block_count
    trace_width = NT * width
    inner_width = own_count * lax.axis_size("sa") * width - 2 * trace_width
    position = lax.axis_index("gx") + lax.axis_index("gy")
    total_steps = lax.axis_size("gx") + lax.axis_size("gy") + block_count - 2
    first_column = lax.axis_index("gy") == 0

    def advance(step, carry):
        east_send, north_send, east_all, north_all, inner_all = carry
        west_in = from_behind(east_send, ("gx", "gy"), lax.axis_size("gy"))
        south_raw = from_behind(north_send, ("gx", "gy"), 1)
        south_in = jnp.where(first_column, jnp.zeros_like(south_raw), south_raw)
        offset = step - position
        active = (offset >= 0) & (offset < block_count)

        def finish(flat):
            east_new = flat[:, :trace_width]
            north_new = flat[:, trace_width : 2 * trace_width]
            inner_new = flat[:, 2 * trace_width :]
            return (east_new, north_new, east_new, north_new, inner_new)

        joined = jnp.concatenate([scaled, west_in, south_in], axis=1)

        def working(state):
            flat = (
                apply_blocks(joined, columns, values, width).astype(jnp.bfloat16).reshape(piece, -1)
            )
            return finish(flat)

        def resting(state):
            return state

        return lax.cond(active, working, resting, carry)

    initial = (
        jnp.zeros((piece, trace_width), jnp.bfloat16),
        jnp.zeros((piece, trace_width), jnp.bfloat16),
        jnp.zeros((rows, trace_width), jnp.bfloat16),
        jnp.zeros((rows, trace_width), jnp.bfloat16),
        jnp.zeros((rows, inner_width), jnp.bfloat16),
    )
    final = lax.fori_loop(0, total_steps, advance, initial)
    return (final[2][None, None], final[3][None, None], final[4][None, None])


def solution(mesh):
    placed = (
        P("gx", "gy", "sa", None),
        P(),
        P("sa"),
        P("gx", "gy", None, None),
        P("gx", "gy", "sa", None, None, None),
    )
    return jax.shard_map(
        on_device,
        mesh=mesh,
        in_specs=placed,
        out_specs=(P("gx", "gy", "sa", None), P("gx", "gy", "sa", None), P("gx", "gy", "sa", None)),
        check_vma=False,
    )
```

profile of v0, /device:TPU:105, one launch (start us, length us, event | category | flops | bytes accessed | tf_op | source)
XLA Modules:
  0.0 502.4 jit_solution(4672858012119289738)
XLA Ops:
  10.3 59.0 %all-gather.2.cloned.1.call-done = bf16[1,1,32,4,128,128]{5,4,3,1,0,2:T(8,128)(2,1)} async-done(((bf16[1,1,8,4,128,128]{5,4,3,1,0,2:T(8,128)(2,1)}), bf16[1,1,32,4,128,128]{5,4,3,1,0,2:T(8,128)(2,1)}) %all-gather.2.cloned.1.call-update) | async-done | bytes 4194320 | tf_op jit(solution)/shard_map/all_gather | solution.py:26
  70.6 424.3 %while.21 = (s32[]{:T(128)}, bf16[8,1536]{1,0:T(8,128)(2,1)}, bf16[8,1536]{1,0:T(8,128)(2,1)}, bf16[8,1536]{1,0:T(8,128)(2,1)S(1)}, bf16[8,1536]{1,0:T(8,128)(2,...) while((s32[]{:T(128)}, bf16[8,1536]{1,0:T(8,128)(2,1)}, ...), condition=%wide.region_3.0_spmd, body=%wide.region_0.3_spmd.sunk | while | flops 33917064 | bytes 5652588 | solution.py:76
  70.6 4.9 collective-permute-start
  75.5 7.7 %collective-permute-start.1 = (bf16[8,1536]{1,0:T(8,128)(2,1)}, bf16[8,1536]{1,0:T(8,128)(2,1)S(1)}, u32[]{:S(2)}, u32[]{:S(2)}) collective-permute-start(bf16[8,1536]{1,0:T(8,128)(2,1)} %get-tuple-element.384), channel_id=1, source_target_pairs={{0,64},{4,68},{8,72},{12,76},{16,80},{20,84},{24,88},{28,92},{32,9... | collective-permute-start | bytes 73736 | tf_op jit(solution)/shard_map/while/body/eval_jaxpr/ppermute | solution.py:12
  83.3 6.6 %collective-permute-done.1 = bf16[8,1536]{1,0:T(8,128)(2,1)S(1)} collective-permute-done((bf16[8,1536]{1,0:T(8,128)(2,1)}, bf16[8,1536]{1,0:T(8,128)(2,1)S(1)}, u32[]{:S(2)}, u32[]{:S(2)}) %collective-permute-start.1) | collective-permute-done | bytes 24608 | tf_op jit(solution)/shard_map/while/body/eval_jaxpr/ppermute | solution.py:12
  89.9 4.0 collective-permute-start
  94.0 6.3 %collective-permute-start.1 = (bf16[8,1536]{1,0:T(8,128)(2,1)}, bf16[8,1536]{1,0:T(8,128)(2,1)S(1)}, u32[]{:S(2)}, u32[]{:S(2)}) collective-permute-start(bf16[8,1536]{1,0:T(8,128)(2,1)} %get-tuple-element.384), channel_id=1, source_target_pairs={{0,64},{4,68},{8,72},{12,76},{16,80},{20,84},{24,88},{28,92},{32,9... | collective-permute-start | bytes 73736 | tf_op jit(solution)/shard_map/while/body/eval_jaxpr/ppermute | solution.py:12
  100.3 8.0 %collective-permute-done.1 = bf16[8,1536]{1,0:T(8,128)(2,1)S(1)} collective-permute-done((bf16[8,1536]{1,0:T(8,128)(2,1)}, bf16[8,1536]{1,0:T(8,128)(2,1)S(1)}, u32[]{:S(2)}, u32[]{:S(2)}) %collective-permute-start.1) | collective-permute-done | bytes 24608 | tf_op jit(solution)/shard_map/while/body/eval_jaxpr/ppermute | solution.py:12
  108.4 3.7 collective-permute-start
  112.1 4.8 collective-permute-start.1
  116.9 9.5 %collective-permute-done.1 = bf16[8,1536]{1,0:T(8,128)(2,1)S(1)} collective-permute-done((bf16[8,1536]{1,0:T(8,128)(2,1)}, bf16[8,1536]{1,0:T(8,128)(2,1)S(1)}, u32[]{:S(2)}, u32[]{:S(2)}) %collective-permute-start.1) | collective-permute-done | bytes 24608 | tf_op jit(solution)/shard_map/while/body/eval_jaxpr/ppermute | solution.py:12
  126.5 3.9 collective-permute-start
  133.3 11.5 %collective-permute-done.1 = bf16[8,1536]{1,0:T(8,128)(2,1)S(1)} collective-permute-done((bf16[8,1536]{1,0:T(8,128)(2,1)}, bf16[8,1536]{1,0:T(8,128)(2,1)S(1)}, u32[]{:S(2)}, u32[]{:S(2)}) %collective-permute-start.1) | collective-permute-done | bytes 24608 | tf_op jit(solution)/shard_map/while/body/eval_jaxpr/ppermute | solution.py:12
  144.8 3.6 collective-permute-start
  150.4 12.4 %collective-permute-done.1 = bf16[8,1536]{1,0:T(8,128)(2,1)S(1)} collective-permute-done((bf16[8,1536]{1,0:T(8,128)(2,1)}, bf16[8,1536]{1,0:T(8,128)(2,1)S(1)}, u32[]{:S(2)}, u32[]{:S(2)}) %collective-permute-start.1) | collective-permute-done | bytes 24608 | tf_op jit(solution)/shard_map/while/body/eval_jaxpr/ppermute | solution.py:12
  167.9 12.4 %collective-permute-done.1 = bf16[8,1536]{1,0:T(8,128)(2,1)S(1)} collective-permute-done((bf16[8,1536]{1,0:T(8,128)(2,1)}, bf16[8,1536]{1,0:T(8,128)(2,1)S(1)}, u32[]{:S(2)}, u32[]{:S(2)}) %collective-permute-start.1) | collective-permute-done | bytes 24608 | tf_op jit(solution)/shard_map/while/body/eval_jaxpr/ppermute | solution.py:12
  180.4 4.3 collective-permute-start
  186.6 12.4 %collective-permute-done.1 = bf16[8,1536]{1,0:T(8,128)(2,1)S(1)} collective-permute-done((bf16[8,1536]{1,0:T(8,128)(2,1)}, bf16[8,1536]{1,0:T(8,128)(2,1)S(1)}, u32[]{:S(2)}, u32[]{:S(2)}) %collective-permute-start.1) | collective-permute-done | bytes 24608 | tf_op jit(solution)/shard_map/while/body/eval_jaxpr/ppermute | solution.py:12
  204.2 12.4 %collective-permute-done.1 = bf16[8,1536]{1,0:T(8,128)(2,1)S(1)} collective-permute-done((bf16[8,1536]{1,0:T(8,128)(2,1)}, bf16[8,1536]{1,0:T(8,128)(2,1)S(1)}, u32[]{:S(2)}, u32[]{:S(2)}) %collective-permute-start.1) | collective-permute-done | bytes 24608 | tf_op jit(solution)/shard_map/while/body/eval_jaxpr/ppermute | solution.py:12
  216.7 4.5 collective-permute-start
  223.2 13.0 %collective-permute-done.1 = bf16[8,1536]{1,0:T(8,128)(2,1)S(1)} collective-permute-done((bf16[8,1536]{1,0:T(8,128)(2,1)}, bf16[8,1536]{1,0:T(8,128)(2,1)S(1)}, u32[]{:S(2)}, u32[]{:S(2)}) %collective-permute-start.1) | collective-permute-done | bytes 24608 | tf_op jit(solution)/shard_map/while/body/eval_jaxpr/ppermute | solution.py:12
  243.3 9.8 %collective-permute-done.1 = bf16[8,1536]{1,0:T(8,128)(2,1)S(1)} collective-permute-done((bf16[8,1536]{1,0:T(8,128)(2,1)}, bf16[8,1536]{1,0:T(8,128)(2,1)S(1)}, u32[]{:S(2)}, u32[]{:S(2)}) %collective-permute-start.1) | collective-permute-done | bytes 24608 | tf_op jit(solution)/shard_map/while/body/eval_jaxpr/ppermute | solution.py:12
  253.1 5.8 %conditional.2 = ((bf16[8,1536]{1,0:T(8,128)(2,1)}, bf16[8,1536]{1,0:T(8,128)(2,1)}, bf16[8,1536]{1,0:T(8,128)(2,1)S(1)}, bf16[8,1536]{1,0:T(8,128)(2,1)S(1)}, bf16[8,1024]{1,0:T(8,128)(2,1)S(1)})) conditional(s32[]{:T(128)} %convert_element_type.32, (bf16[8,1536]{1,0:T(8,128)(2,1)}, bf16[8,1536]{1,0:T(8,128)(2,1)}, bf16[8,1536]{1,0:T(8,128)(2,1)S(1)}, ...), branch_computations={%region_1.1_spmd, %region_2.2_spmd} | conditional | flops 33720448 | bytes 5283632 | solution.py:67
  262.9 12.7 %collective-permute-done.1 = bf16[8,1536]{1,0:T(8,128)(2,1)S(1)} collective-permute-done((bf16[8,1536]{1,0:T(8,128)(2,1)}, bf16[8,1536]{1,0:T(8,128)(2,1)S(1)}, u32[]{:S(2)}, u32[]{:S(2)}) %collective-permute-start.1) | collective-permute-done | bytes 24608 | tf_op jit(solution)/shard_map/while/body/eval_jaxpr/ppermute | solution.py:12
  275.6 4.6 collective-permute-start
  280.2 3.9 collective-permute-start.1
  284.2 10.4 %collective-permute-done.1 = bf16[8,1536]{1,0:T(8,128)(2,1)S(1)} collective-permute-done((bf16[8,1536]{1,0:T(8,128)(2,1)}, bf16[8,1536]{1,0:T(8,128)(2,1)S(1)}, u32[]{:S(2)}, u32[]{:S(2)}) %collective-permute-start.1) | collective-permute-done | bytes 24608 | tf_op jit(solution)/shard_map/while/body/eval_jaxpr/ppermute | solution.py:12
  297.7 6.6 %collective-permute-start.1 = (bf16[8,1536]{1,0:T(8,128)(2,1)}, bf16[8,1536]{1,0:T(8,128)(2,1)S(1)}, u32[]{:S(2)}, u32[]{:S(2)}) collective-permute-start(bf16[8,1536]{1,0:T(8,128)(2,1)} %get-tuple-element.384), channel_id=1, source_target_pairs={{0,64},{4,68},{8,72},{12,76},{16,80},{20,84},{24,88},{28,92},{32,9... | collective-permute-start | bytes 73736 | tf_op jit(solution)/shard_map/while/body/eval_jaxpr/ppermute | solution.py:12
  304.3 7.9 %collective-permute-done.1 = bf16[8,1536]{1,0:T(8,128)(2,1)S(1)} collective-permute-done((bf16[8,1536]{1,0:T(8,128)(2,1)}, bf16[8,1536]{1,0:T(8,128)(2,1)S(1)}, u32[]{:S(2)}, u32[]{:S(2)}) %collective-permute-start.1) | collective-permute-done | bytes 24608 | tf_op jit(solution)/shard_map/while/body/eval_jaxpr/ppermute | solution.py:12
  312.2 5.0 collective-permute-start
  317.2 3.8 collective-permute-start.1
  321.1 10.5 %collective-permute-done.1 = bf16[8,1536]{1,0:T(8,128)(2,1)S(1)} collective-permute-done((bf16[8,1536]{1,0:T(8,128)(2,1)}, bf16[8,1536]{1,0:T(8,128)(2,1)S(1)}, u32[]{:S(2)}, u32[]{:S(2)}) %collective-permute-start.1) | collective-permute-done | bytes 24608 | tf_op jit(solution)/shard_map/while/body/eval_jaxpr/ppermute | solution.py:12
  331.6 3.9 collective-permute-start
  338.6 11.3 %collective-permute-done.1 = bf16[8,1536]{1,0:T(8,128)(2,1)S(1)} collective-permute-done((bf16[8,1536]{1,0:T(8,128)(2,1)}, bf16[8,1536]{1,0:T(8,128)(2,1)S(1)}, u32[]{:S(2)}, u32[]{:S(2)}) %collective-permute-start.1) | collective-permute-done | bytes 24608 | tf_op jit(solution)/shard_map/while/body/eval_jaxpr/ppermute | solution.py:12
  349.9 3.6 collective-permute-start
  355.5 12.7 %collective-permute-done.1 = bf16[8,1536]{1,0:T(8,128)(2,1)S(1)} collective-permute-done((bf16[8,1536]{1,0:T(8,128)(2,1)}, bf16[8,1536]{1,0:T(8,128)(2,1)S(1)}, u32[]{:S(2)}, u32[]{:S(2)}) %collective-permute-start.1) | collective-permute-done | bytes 24608 | tf_op jit(solution)/shard_map/while/body/eval_jaxpr/ppermute | solution.py:12
  371.4 3.5 collective-permute-start.1
  374.9 10.9 %collective-permute-done.1 = bf16[8,1536]{1,0:T(8,128)(2,1)S(1)} collective-permute-done((bf16[8,1536]{1,0:T(8,128)(2,1)}, bf16[8,1536]{1,0:T(8,128)(2,1)S(1)}, u32[]{:S(2)}, u32[]{:S(2)}) %collective-permute-start.1) | collective-permute-done | bytes 24608 | tf_op jit(solution)/shard_map/while/body/eval_jaxpr/ppermute | solution.py:12
  385.8 3.4 collective-permute-start
  391.6 12.1 %collective-permute-done.1 = bf16[8,1536]{1,0:T(8,128)(2,1)S(1)} collective-permute-done((bf16[8,1536]{1,0:T(8,128)(2,1)}, bf16[8,1536]{1,0:T(8,128)(2,1)S(1)}, u32[]{:S(2)}, u32[]{:S(2)}) %collective-permute-start.1) | collective-permute-done | bytes 24608 | tf_op jit(solution)/shard_map/while/body/eval_jaxpr/ppermute | solution.py:12
  408.7 12.5 %collective-permute-done.1 = bf16[8,1536]{1,0:T(8,128)(2,1)S(1)} collective-permute-done((bf16[8,1536]{1,0:T(8,128)(2,1)}, bf16[8,1536]{1,0:T(8,128)(2,1)S(1)}, u32[]{:S(2)}, u32[]{:S(2)}) %collective-permute-start.1) | collective-permute-done | bytes 24608 | tf_op jit(solution)/shard_map/while/body/eval_jaxpr/ppermute | solution.py:12
  426.8 12.0 %collective-permute-done.1 = bf16[8,1536]{1,0:T(8,128)(2,1)S(1)} collective-permute-done((bf16[8,1536]{1,0:T(8,128)(2,1)}, bf16[8,1536]{1,0:T(8,128)(2,1)S(1)}, u32[]{:S(2)}, u32[]{:S(2)}) %collective-permute-start.1) | collective-permute-done | bytes 24608 | tf_op jit(solution)/shard_map/while/body/eval_jaxpr/ppermute | solution.py:12
  438.8 3.2 collective-permute-start
  444.3 12.5 %collective-permute-done.1 = bf16[8,1536]{1,0:T(8,128)(2,1)S(1)} collective-permute-done((bf16[8,1536]{1,0:T(8,128)(2,1)}, bf16[8,1536]{1,0:T(8,128)(2,1)S(1)}, u32[]{:S(2)}, u32[]{:S(2)}) %collective-permute-start.1) | collective-permute-done | bytes 24608 | tf_op jit(solution)/shard_map/while/body/eval_jaxpr/ppermute | solution.py:12
  456.8 5.3 %collective-permute-start = (bf16[8,1536]{1,0:T(8,128)(2,1)}, bf16[8,1536]{1,0:T(8,128)(2,1)S(1)}, u32[]{:S(2)}, u32[]{:S(2)}) collective-permute-start(bf16[8,1536]{1,0:T(8,128)(2,1)} %get-tuple-element.385), channel_id=1, source_target_pairs={{0,4},{4,8},{8,12},{12,16},{16,20},{20,24},{24,28},{28,32},{32,36}... | collective-permute-start | bytes 73736 | tf_op jit(solution)/shard_map/while/body/eval_jaxpr/ppermute | solution.py:12
  464.1 12.4 %collective-permute-done.1 = bf16[8,1536]{1,0:T(8,128)(2,1)S(1)} collective-permute-done((bf16[8,1536]{1,0:T(8,128)(2,1)}, bf16[8,1536]{1,0:T(8,128)(2,1)S(1)}, u32[]{:S(2)}, u32[]{:S(2)}) %collective-permute-start.1) | collective-permute-done | bytes 24608 | tf_op jit(solution)/shard_map/while/body/eval_jaxpr/ppermute | solution.py:12
  476.5 4.0 collective-permute-start
  482.5 12.4 %collective-permute-done.1 = bf16[8,1536]{1,0:T(8,128)(2,1)S(1)} collective-permute-done((bf16[8,1536]{1,0:T(8,128)(2,1)}, bf16[8,1536]{1,0:T(8,128)(2,1)S(1)}, u32[]{:S(2)}, u32[]{:S(2)}) %collective-permute-start.1) | collective-permute-done | bytes 24608 | tf_op jit(solution)/shard_map/while/body/eval_jaxpr/ppermute | solution.py:12
  (143 shorter events, 71.0 us)
Async XLA Ops:
  7.2 1.5 copy-start
  7.2 62.2 %all-gather.2.cloned.1.call-start = ((), (), s32[]{:S(2)}) async-start(), calls=%async_computation | async-start | bytes 5242880 | tf_op jit(solution)/shard_map/all_gather | solution.py:26
  70.6 12.7 %collective-permute-start = (bf16[8,1536]{1,0:T(8,128)(2,1)}, bf16[8,1536]{1,0:T(8,128)(2,1)S(1)}, u32[]{:S(2)}, u32[]{:S(2)}) collective-permute-start(bf16[8,1536]{1,0:T(8,128)(2,1)} %get-tuple-element.385), channel_id=1, source_target_pairs={{0,4},{4,8},{8,12},{12,16},{16,20},{20,24},{24,28},{28,32},{32,36}... | collective-permute-start | bytes 73736 | tf_op jit(solution)/shard_map/while/body/eval_jaxpr/ppermute | solution.py:12
  75.5 14.4 %collective-permute-start.1 = (bf16[8,1536]{1,0:T(8,128)(2,1)}, bf16[8,1536]{1,0:T(8,128)(2,1)S(1)}, u32[]{:S(2)}, u32[]{:S(2)}) collective-permute-start(bf16[8,1536]{1,0:T(8,128)(2,1)} %get-tuple-element.384), channel_id=1, source_target_pairs={{0,64},{4,68},{8,72},{12,76},{16,80},{20,84},{24,88},{28,92},{32,9... | collective-permute-start | bytes 73736 | tf_op jit(solution)/shard_map/while/body/eval_jaxpr/ppermute | solution.py:12
  89.9 10.4 %collective-permute-start = (bf16[8,1536]{1,0:T(8,128)(2,1)}, bf16[8,1536]{1,0:T(8,128)(2,1)S(1)}, u32[]{:S(2)}, u32[]{:S(2)}) collective-permute-start(bf16[8,1536]{1,0:T(8,128)(2,1)} %get-tuple-element.385), channel_id=1, source_target_pairs={{0,4},{4,8},{8,12},{12,16},{16,20},{20,24},{24,28},{28,32},{32,36}... | collective-permute-start | bytes 73736 | tf_op jit(solution)/shard_map/while/body/eval_jaxpr/ppermute | solution.py:12
  94.0 14.4 %collective-permute-start.1 = (bf16[8,1536]{1,0:T(8,128)(2,1)}, bf16[8,1536]{1,0:T(8,128)(2,1)S(1)}, u32[]{:S(2)}, u32[]{:S(2)}) collective-permute-start(bf16[8,1536]{1,0:T(8,128)(2,1)} %get-tuple-element.384), channel_id=1, source_target_pairs={{0,64},{4,68},{8,72},{12,76},{16,80},{20,84},{24,88},{28,92},{32,9... | collective-permute-start | bytes 73736 | tf_op jit(solution)/shard_map/while/body/eval_jaxpr/ppermute | solution.py:12
  108.4 8.5 %collective-permute-start = (bf16[8,1536]{1,0:T(8,128)(2,1)}, bf16[8,1536]{1,0:T(8,128)(2,1)S(1)}, u32[]{:S(2)}, u32[]{:S(2)}) collective-permute-start(bf16[8,1536]{1,0:T(8,128)(2,1)} %get-tuple-element.385), channel_id=1, source_target_pairs={{0,4},{4,8},{8,12},{12,16},{16,20},{20,24},{24,28},{28,32},{32,36}... | collective-permute-start | bytes 73736 | tf_op jit(solution)/shard_map/while/body/eval_jaxpr/ppermute | solution.py:12
  112.1 14.4 %collective-permute-start.1 = (bf16[8,1536]{1,0:T(8,128)(2,1)}, bf16[8,1536]{1,0:T(8,128)(2,1)S(1)}, u32[]{:S(2)}, u32[]{:S(2)}) collective-permute-start(bf16[8,1536]{1,0:T(8,128)(2,1)} %get-tuple-element.384), channel_id=1, source_target_pairs={{0,64},{4,68},{8,72},{12,76},{16,80},{20,84},{24,88},{28,92},{32,9... | collective-permute-start | bytes 73736 | tf_op jit(solution)/shard_map/while/body/eval_jaxpr/ppermute | solution.py:12
  126.5 6.8 %collective-permute-start = (bf16[8,1536]{1,0:T(8,128)(2,1)}, bf16[8,1536]{1,0:T(8,128)(2,1)S(1)}, u32[]{:S(2)}, u32[]{:S(2)}) collective-permute-start(bf16[8,1536]{1,0:T(8,128)(2,1)} %get-tuple-element.385), channel_id=1, source_target_pairs={{0,4},{4,8},{8,12},{12,16},{16,20},{20,24},{24,28},{28,32},{32,36}... | collective-permute-start | bytes 73736 | tf_op jit(solution)/shard_map/while/body/eval_jaxpr/ppermute | solution.py:12
  130.4 14.4 %collective-permute-start.1 = (bf16[8,1536]{1,0:T(8,128)(2,1)}, bf16[8,1536]{1,0:T(8,128)(2,1)S(1)}, u32[]{:S(2)}, u32[]{:S(2)}) collective-permute-start(bf16[8,1536]{1,0:T(8,128)(2,1)} %get-tuple-element.384), channel_id=1, source_target_pairs={{0,64},{4,68},{8,72},{12,76},{16,80},{20,84},{24,88},{28,92},{32,9... | collective-permute-start | bytes 73736 | tf_op jit(solution)/shard_map/while/body/eval_jaxpr/ppermute | solution.py:12
  144.8 5.5 %collective-permute-start = (bf16[8,1536]{1,0:T(8,128)(2,1)}, bf16[8,1536]{1,0:T(8,128)(2,1)S(1)}, u32[]{:S(2)}, u32[]{:S(2)}) collective-permute-start(bf16[8,1536]{1,0:T(8,128)(2,1)} %get-tuple-element.385), channel_id=1, source_target_pairs={{0,4},{4,8},{8,12},{12,16},{16,20},{20,24},{24,28},{28,32},{32,36}... | collective-permute-start | bytes 73736 | tf_op jit(solution)/shard_map/while/body/eval_jaxpr/ppermute | solution.py:12
  148.4 14.4 %collective-permute-start.1 = (bf16[8,1536]{1,0:T(8,128)(2,1)}, bf16[8,1536]{1,0:T(8,128)(2,1)S(1)}, u32[]{:S(2)}, u32[]{:S(2)}) collective-permute-start(bf16[8,1536]{1,0:T(8,128)(2,1)} %get-tuple-element.384), channel_id=1, source_target_pairs={{0,64},{4,68},{8,72},{12,76},{16,80},{20,84},{24,88},{28,92},{32,9... | collective-permute-start | bytes 73736 | tf_op jit(solution)/shard_map/while/body/eval_jaxpr/ppermute | solution.py:12
  162.8 5.1 %collective-permute-start = (bf16[8,1536]{1,0:T(8,128)(2,1)}, bf16[8,1536]{1,0:T(8,128)(2,1)S(1)}, u32[]{:S(2)}, u32[]{:S(2)}) collective-permute-start(bf16[8,1536]{1,0:T(8,128)(2,1)} %get-tuple-element.385), channel_id=1, source_target_pairs={{0,4},{4,8},{8,12},{12,16},{16,20},{20,24},{24,28},{28,32},{32,36}... | collective-permute-start | bytes 73736 | tf_op jit(solution)/shard_map/while/body/eval_jaxpr/ppermute | solution.py:12
  166.0 14.4 %collective-permute-start.1 = (bf16[8,1536]{1,0:T(8,128)(2,1)}, bf16[8,1536]{1,0:T(8,128)(2,1)S(1)}, u32[]{:S(2)}, u32[]{:S(2)}) collective-permute-start(bf16[8,1536]{1,0:T(8,128)(2,1)} %get-tuple-element.384), channel_id=1, source_target_pairs={{0,64},{4,68},{8,72},{12,76},{16,80},{20,84},{24,88},{28,92},{32,9... | collective-permute-start | bytes 73736 | tf_op jit(solution)/shard_map/while/body/eval_jaxpr/ppermute | solution.py:12
  180.4 6.3 %collective-permute-start = (bf16[8,1536]{1,0:T(8,128)(2,1)}, bf16[8,1536]{1,0:T(8,128)(2,1)S(1)}, u32[]{:S(2)}, u32[]{:S(2)}) collective-permute-start(bf16[8,1536]{1,0:T(8,128)(2,1)} %get-tuple-element.385), channel_id=1, source_target_pairs={{0,4},{4,8},{8,12},{12,16},{16,20},{20,24},{24,28},{28,32},{32,36}... | collective-permute-start | bytes 73736 | tf_op jit(solution)/shard_map/while/body/eval_jaxpr/ppermute | solution.py:12
  184.7 14.4 %collective-permute-start.1 = (bf16[8,1536]{1,0:T(8,128)(2,1)}, bf16[8,1536]{1,0:T(8,128)(2,1)S(1)}, u32[]{:S(2)}, u32[]{:S(2)}) collective-permute-start(bf16[8,1536]{1,0:T(8,128)(2,1)} %get-tuple-element.384), channel_id=1, source_target_pairs={{0,64},{4,68},{8,72},{12,76},{16,80},{20,84},{24,88},{28,92},{32,9... | collective-permute-start | bytes 73736 | tf_op jit(solution)/shard_map/while/body/eval_jaxpr/ppermute | solution.py:12
  199.1 5.1 %collective-permute-start = (bf16[8,1536]{1,0:T(8,128)(2,1)}, bf16[8,1536]{1,0:T(8,128)(2,1)S(1)}, u32[]{:S(2)}, u32[]{:S(2)}) collective-permute-start(bf16[8,1536]{1,0:T(8,128)(2,1)} %get-tuple-element.385), channel_id=1, source_target_pairs={{0,4},{4,8},{8,12},{12,16},{16,20},{20,24},{24,28},{28,32},{32,36}... | collective-permute-start | bytes 73736 | tf_op jit(solution)/shard_map/while/body/eval_jaxpr/ppermute | solution.py:12
  202.2 14.4 %collective-permute-start.1 = (bf16[8,1536]{1,0:T(8,128)(2,1)}, bf16[8,1536]{1,0:T(8,128)(2,1)S(1)}, u32[]{:S(2)}, u32[]{:S(2)}) collective-permute-start(bf16[8,1536]{1,0:T(8,128)(2,1)} %get-tuple-element.384), channel_id=1, source_target_pairs={{0,64},{4,68},{8,72},{12,76},{16,80},{20,84},{24,88},{28,92},{32,9... | collective-permute-start | bytes 73736 | tf_op jit(solution)/shard_map/while/body/eval_jaxpr/ppermute | solution.py:12
  216.7 6.5 %collective-permute-start = (bf16[8,1536]{1,0:T(8,128)(2,1)}, bf16[8,1536]{1,0:T(8,128)(2,1)S(1)}, u32[]{:S(2)}, u32[]{:S(2)}) collective-permute-start(bf16[8,1536]{1,0:T(8,128)(2,1)} %get-tuple-element.385), channel_id=1, source_target_pairs={{0,4},{4,8},{8,12},{12,16},{16,20},{20,24},{24,28},{28,32},{32,36}... | collective-permute-start | bytes 73736 | tf_op jit(solution)/shard_map/while/body/eval_jaxpr/ppermute | solution.py:12
  221.2 14.9 %collective-permute-start.1 = (bf16[8,1536]{1,0:T(8,128)(2,1)}, bf16[8,1536]{1,0:T(8,128)(2,1)S(1)}, u32[]{:S(2)}, u32[]{:S(2)}) collective-permute-start(bf16[8,1536]{1,0:T(8,128)(2,1)} %get-tuple-element.384), channel_id=1, source_target_pairs={{0,64},{4,68},{8,72},{12,76},{16,80},{20,84},{24,88},{28,92},{32,9... | collective-permute-start | bytes 73736 | tf_op jit(solution)/shard_map/while/body/eval_jaxpr/ppermute | solution.py:12
  236.1 7.2 %collective-permute-start = (bf16[8,1536]{1,0:T(8,128)(2,1)}, bf16[8,1536]{1,0:T(8,128)(2,1)S(1)}, u32[]{:S(2)}, u32[]{:S(2)}) collective-permute-start(bf16[8,1536]{1,0:T(8,128)(2,1)} %get-tuple-element.385), channel_id=1, source_target_pairs={{0,4},{4,8},{8,12},{12,16},{16,20},{20,24},{24,28},{28,32},{32,36}... | collective-permute-start | bytes 73736 | tf_op jit(solution)/shard_map/while/body/eval_jaxpr/ppermute | solution.py:12
  238.7 14.4 %collective-permute-start.1 = (bf16[8,1536]{1,0:T(8,128)(2,1)}, bf16[8,1536]{1,0:T(8,128)(2,1)S(1)}, u32[]{:S(2)}, u32[]{:S(2)}) collective-permute-start(bf16[8,1536]{1,0:T(8,128)(2,1)} %get-tuple-element.384), channel_id=1, source_target_pairs={{0,64},{4,68},{8,72},{12,76},{16,80},{20,84},{24,88},{28,92},{32,9... | collective-permute-start | bytes 73736 | tf_op jit(solution)/shard_map/while/body/eval_jaxpr/ppermute | solution.py:12
  259.0 3.9 collective-permute-start
  260.9 14.7 %collective-permute-start.1 = (bf16[8,1536]{1,0:T(8,128)(2,1)}, bf16[8,1536]{1,0:T(8,128)(2,1)S(1)}, u32[]{:S(2)}, u32[]{:S(2)}) collective-permute-start(bf16[8,1536]{1,0:T(8,128)(2,1)} %get-tuple-element.384), channel_id=1, source_target_pairs={{0,64},{4,68},{8,72},{12,76},{16,80},{20,84},{24,88},{28,92},{32,9... | collective-permute-start | bytes 73736 | tf_op jit(solution)/shard_map/while/body/eval_jaxpr/ppermute | solution.py:12
  275.6 8.6 %collective-permute-start = (bf16[8,1536]{1,0:T(8,128)(2,1)}, bf16[8,1536]{1,0:T(8,128)(2,1)S(1)}, u32[]{:S(2)}, u32[]{:S(2)}) collective-permute-start(bf16[8,1536]{1,0:T(8,128)(2,1)} %get-tuple-element.385), channel_id=1, source_target_pairs={{0,4},{4,8},{8,12},{12,16},{16,20},{20,24},{24,28},{28,32},{32,36}... | collective-permute-start | bytes 73736 | tf_op jit(solution)/shard_map/while/body/eval_jaxpr/ppermute | solution.py:12
  280.2 14.4 %collective-permute-start.1 = (bf16[8,1536]{1,0:T(8,128)(2,1)}, bf16[8,1536]{1,0:T(8,128)(2,1)S(1)}, u32[]{:S(2)}, u32[]{:S(2)}) collective-permute-start(bf16[8,1536]{1,0:T(8,128)(2,1)} %get-tuple-element.384), channel_id=1, source_target_pairs={{0,64},{4,68},{8,72},{12,76},{16,80},{20,84},{24,88},{28,92},{32,9... | collective-permute-start | bytes 73736 | tf_op jit(solution)/shard_map/while/body/eval_jaxpr/ppermute | solution.py:12
  294.6 9.7 %collective-permute-start = (bf16[8,1536]{1,0:T(8,128)(2,1)}, bf16[8,1536]{1,0:T(8,128)(2,1)S(1)}, u32[]{:S(2)}, u32[]{:S(2)}) collective-permute-start(bf16[8,1536]{1,0:T(8,128)(2,1)} %get-tuple-element.385), channel_id=1, source_target_pairs={{0,4},{4,8},{8,12},{12,16},{16,20},{20,24},{24,28},{28,32},{32,36}... | collective-permute-start | bytes 73736 | tf_op jit(solution)/shard_map/while/body/eval_jaxpr/ppermute | solution.py:12
  297.7 14.5 %collective-permute-start.1 = (bf16[8,1536]{1,0:T(8,128)(2,1)}, bf16[8,1536]{1,0:T(8,128)(2,1)S(1)}, u32[]{:S(2)}, u32[]{:S(2)}) collective-permute-start(bf16[8,1536]{1,0:T(8,128)(2,1)} %get-tuple-element.384), channel_id=1, source_target_pairs={{0,64},{4,68},{8,72},{12,76},{16,80},{20,84},{24,88},{28,92},{32,9... | collective-permute-start | bytes 73736 | tf_op jit(solution)/shard_map/while/body/eval_jaxpr/ppermute | solution.py:12
  312.2 8.8 %collective-permute-start = (bf16[8,1536]{1,0:T(8,128)(2,1)}, bf16[8,1536]{1,0:T(8,128)(2,1)S(1)}, u32[]{:S(2)}, u32[]{:S(2)}) collective-permute-start(bf16[8,1536]{1,0:T(8,128)(2,1)} %get-tuple-element.385), channel_id=1, source_target_pairs={{0,4},{4,8},{8,12},{12,16},{16,20},{20,24},{24,28},{28,32},{32,36}... | collective-permute-start | bytes 73736 | tf_op jit(solution)/shard_map/while/body/eval_jaxpr/ppermute | solution.py:12
  317.2 14.4 %collective-permute-start.1 = (bf16[8,1536]{1,0:T(8,128)(2,1)}, bf16[8,1536]{1,0:T(8,128)(2,1)S(1)}, u32[]{:S(2)}, u32[]{:S(2)}) collective-permute-start(bf16[8,1536]{1,0:T(8,128)(2,1)} %get-tuple-element.384), channel_id=1, source_target_pairs={{0,64},{4,68},{8,72},{12,76},{16,80},{20,84},{24,88},{28,92},{32,9... | collective-permute-start | bytes 73736 | tf_op jit(solution)/shard_map/while/body/eval_jaxpr/ppermute | solution.py:12
  331.6 7.0 %collective-permute-start = (bf16[8,1536]{1,0:T(8,128)(2,1)}, bf16[8,1536]{1,0:T(8,128)(2,1)S(1)}, u32[]{:S(2)}, u32[]{:S(2)}) collective-permute-start(bf16[8,1536]{1,0:T(8,128)(2,1)} %get-tuple-element.385), channel_id=1, source_target_pairs={{0,4},{4,8},{8,12},{12,16},{16,20},{20,24},{24,28},{28,32},{32,36}... | collective-permute-start | bytes 73736 | tf_op jit(solution)/shard_map/while/body/eval_jaxpr/ppermute | solution.py:12
  335.5 14.5 %collective-permute-start.1 = (bf16[8,1536]{1,0:T(8,128)(2,1)}, bf16[8,1536]{1,0:T(8,128)(2,1)S(1)}, u32[]{:S(2)}, u32[]{:S(2)}) collective-permute-start(bf16[8,1536]{1,0:T(8,128)(2,1)} %get-tuple-element.384), channel_id=1, source_target_pairs={{0,64},{4,68},{8,72},{12,76},{16,80},{20,84},{24,88},{28,92},{32,9... | collective-permute-start | bytes 73736 | tf_op jit(solution)/shard_map/while/body/eval_jaxpr/ppermute | solution.py:12
  349.9 5.6 %collective-permute-start = (bf16[8,1536]{1,0:T(8,128)(2,1)}, bf16[8,1536]{1,0:T(8,128)(2,1)S(1)}, u32[]{:S(2)}, u32[]{:S(2)}) collective-permute-start(bf16[8,1536]{1,0:T(8,128)(2,1)} %get-tuple-element.385), channel_id=1, source_target_pairs={{0,4},{4,8},{8,12},{12,16},{16,20},{20,24},{24,28},{28,32},{32,36}... | collective-permute-start | bytes 73736 | tf_op jit(solution)/shard_map/while/body/eval_jaxpr/ppermute | solution.py:12
  353.6 14.7 %collective-permute-start.1 = (bf16[8,1536]{1,0:T(8,128)(2,1)}, bf16[8,1536]{1,0:T(8,128)(2,1)S(1)}, u32[]{:S(2)}, u32[]{:S(2)}) collective-permute-start(bf16[8,1536]{1,0:T(8,128)(2,1)} %get-tuple-element.384), channel_id=1, source_target_pairs={{0,64},{4,68},{8,72},{12,76},{16,80},{20,84},{24,88},{28,92},{32,9... | collective-permute-start | bytes 73736 | tf_op jit(solution)/shard_map/while/body/eval_jaxpr/ppermute | solution.py:12
  368.2 6.6 %collective-permute-start = (bf16[8,1536]{1,0:T(8,128)(2,1)}, bf16[8,1536]{1,0:T(8,128)(2,1)S(1)}, u32[]{:S(2)}, u32[]{:S(2)}) collective-permute-start(bf16[8,1536]{1,0:T(8,128)(2,1)} %get-tuple-element.385), channel_id=1, source_target_pairs={{0,4},{4,8},{8,12},{12,16},{16,20},{20,24},{24,28},{28,32},{32,36}... | collective-permute-start | bytes 73736 | tf_op jit(solution)/shard_map/while/body/eval_jaxpr/ppermute | solution.py:12
  371.4 14.4 %collective-permute-start.1 = (bf16[8,1536]{1,0:T(8,128)(2,1)}, bf16[8,1536]{1,0:T(8,128)(2,1)S(1)}, u32[]{:S(2)}, u32[]{:S(2)}) collective-permute-start(bf16[8,1536]{1,0:T(8,128)(2,1)} %get-tuple-element.384), channel_id=1, source_target_pairs={{0,64},{4,68},{8,72},{12,76},{16,80},{20,84},{24,88},{28,92},{32,9... | collective-permute-start | bytes 73736 | tf_op jit(solution)/shard_map/while/body/eval_jaxpr/ppermute | solution.py:12
  385.8 5.7 %collective-permute-start = (bf16[8,1536]{1,0:T(8,128)(2,1)}, bf16[8,1536]{1,0:T(8,128)(2,1)S(1)}, u32[]{:S(2)}, u32[]{:S(2)}) collective-permute-start(bf16[8,1536]{1,0:T(8,128)(2,1)} %get-tuple-element.385), channel_id=1, source_target_pairs={{0,4},{4,8},{8,12},{12,16},{16,20},{20,24},{24,28},{28,32},{32,36}... | collective-permute-start | bytes 73736 | tf_op jit(solution)/shard_map/while/body/eval_jaxpr/ppermute | solution.py:12
  389.2 14.4 %collective-permute-start.1 = (bf16[8,1536]{1,0:T(8,128)(2,1)}, bf16[8,1536]{1,0:T(8,128)(2,1)S(1)}, u32[]{:S(2)}, u32[]{:S(2)}) collective-permute-start(bf16[8,1536]{1,0:T(8,128)(2,1)} %get-tuple-element.384), channel_id=1, source_target_pairs={{0,64},{4,68},{8,72},{12,76},{16,80},{20,84},{24,88},{28,92},{32,9... | collective-permute-start | bytes 73736 | tf_op jit(solution)/shard_map/while/body/eval_jaxpr/ppermute | solution.py:12
  403.6 5.1 %collective-permute-start = (bf16[8,1536]{1,0:T(8,128)(2,1)}, bf16[8,1536]{1,0:T(8,128)(2,1)S(1)}, u32[]{:S(2)}, u32[]{:S(2)}) collective-permute-start(bf16[8,1536]{1,0:T(8,128)(2,1)} %get-tuple-element.385), channel_id=1, source_target_pairs={{0,4},{4,8},{8,12},{12,16},{16,20},{20,24},{24,28},{28,32},{32,36}... | collective-permute-start | bytes 73736 | tf_op jit(solution)/shard_map/while/body/eval_jaxpr/ppermute | solution.py:12
  406.8 14.5 %collective-permute-start.1 = (bf16[8,1536]{1,0:T(8,128)(2,1)}, bf16[8,1536]{1,0:T(8,128)(2,1)S(1)}, u32[]{:S(2)}, u32[]{:S(2)}) collective-permute-start(bf16[8,1536]{1,0:T(8,128)(2,1)} %get-tuple-element.384), channel_id=1, source_target_pairs={{0,64},{4,68},{8,72},{12,76},{16,80},{20,84},{24,88},{28,92},{32,9... | collective-permute-start | bytes 73736 | tf_op jit(solution)/shard_map/while/body/eval_jaxpr/ppermute | solution.py:12
  421.2 5.5 %collective-permute-start = (bf16[8,1536]{1,0:T(8,128)(2,1)}, bf16[8,1536]{1,0:T(8,128)(2,1)S(1)}, u32[]{:S(2)}, u32[]{:S(2)}) collective-permute-start(bf16[8,1536]{1,0:T(8,128)(2,1)} %get-tuple-element.385), channel_id=1, source_target_pairs={{0,4},{4,8},{8,12},{12,16},{16,20},{20,24},{24,28},{28,32},{32,36}... | collective-permute-start | bytes 73736 | tf_op jit(solution)/shard_map/while/body/eval_jaxpr/ppermute | solution.py:12
  424.4 14.4 %collective-permute-start.1 = (bf16[8,1536]{1,0:T(8,128)(2,1)}, bf16[8,1536]{1,0:T(8,128)(2,1)S(1)}, u32[]{:S(2)}, u32[]{:S(2)}) collective-permute-start(bf16[8,1536]{1,0:T(8,128)(2,1)} %get-tuple-element.384), channel_id=1, source_target_pairs={{0,64},{4,68},{8,72},{12,76},{16,80},{20,84},{24,88},{28,92},{32,9... | collective-permute-start | bytes 73736 | tf_op jit(solution)/shard_map/while/body/eval_jaxpr/ppermute | solution.py:12
  438.8 5.4 %collective-permute-start = (bf16[8,1536]{1,0:T(8,128)(2,1)}, bf16[8,1536]{1,0:T(8,128)(2,1)S(1)}, u32[]{:S(2)}, u32[]{:S(2)}) collective-permute-start(bf16[8,1536]{1,0:T(8,128)(2,1)} %get-tuple-element.385), channel_id=1, source_target_pairs={{0,4},{4,8},{8,12},{12,16},{16,20},{20,24},{24,28},{28,32},{32,36}... | collective-permute-start | bytes 73736 | tf_op jit(solution)/shard_map/while/body/eval_jaxpr/ppermute | solution.py:12
  442.1 14.7 %collective-permute-start.1 = (bf16[8,1536]{1,0:T(8,128)(2,1)}, bf16[8,1536]{1,0:T(8,128)(2,1)S(1)}, u32[]{:S(2)}, u32[]{:S(2)}) collective-permute-start(bf16[8,1536]{1,0:T(8,128)(2,1)} %get-tuple-element.384), channel_id=1, source_target_pairs={{0,64},{4,68},{8,72},{12,76},{16,80},{20,84},{24,88},{28,92},{32,9... | collective-permute-start | bytes 73736 | tf_op jit(solution)/shard_map/while/body/eval_jaxpr/ppermute | solution.py:12
  456.8 7.3 %collective-permute-start = (bf16[8,1536]{1,0:T(8,128)(2,1)}, bf16[8,1536]{1,0:T(8,128)(2,1)S(1)}, u32[]{:S(2)}, u32[]{:S(2)}) collective-permute-start(bf16[8,1536]{1,0:T(8,128)(2,1)} %get-tuple-element.385), channel_id=1, source_target_pairs={{0,4},{4,8},{8,12},{12,16},{16,20},{20,24},{24,28},{28,32},{32,36}... | collective-permute-start | bytes 73736 | tf_op jit(solution)/shard_map/while/body/eval_jaxpr/ppermute | solution.py:12
  462.1 14.4 %collective-permute-start.1 = (bf16[8,1536]{1,0:T(8,128)(2,1)}, bf16[8,1536]{1,0:T(8,128)(2,1)S(1)}, u32[]{:S(2)}, u32[]{:S(2)}) collective-permute-start(bf16[8,1536]{1,0:T(8,128)(2,1)} %get-tuple-element.384), channel_id=1, source_target_pairs={{0,64},{4,68},{8,72},{12,76},{16,80},{20,84},{24,88},{28,92},{32,9... | collective-permute-start | bytes 73736 | tf_op jit(solution)/shard_map/while/body/eval_jaxpr/ppermute | solution.py:12
  476.5 6.0 %collective-permute-start = (bf16[8,1536]{1,0:T(8,128)(2,1)}, bf16[8,1536]{1,0:T(8,128)(2,1)S(1)}, u32[]{:S(2)}, u32[]{:S(2)}) collective-permute-start(bf16[8,1536]{1,0:T(8,128)(2,1)} %get-tuple-element.385), channel_id=1, source_target_pairs={{0,4},{4,8},{8,12},{12,16},{16,20},{20,24},{24,28},{28,32},{32,36}... | collective-permute-start | bytes 73736 | tf_op jit(solution)/shard_map/while/body/eval_jaxpr/ppermute | solution.py:12
  480.5 14.4 %collective-permute-start.1 = (bf16[8,1536]{1,0:T(8,128)(2,1)}, bf16[8,1536]{1,0:T(8,128)(2,1)S(1)}, u32[]{:S(2)}, u32[]{:S(2)}) collective-permute-start(bf16[8,1536]{1,0:T(8,128)(2,1)} %get-tuple-element.384), channel_id=1, source_target_pairs={{0,64},{4,68},{8,72},{12,76},{16,80},{20,84},{24,88},{28,92},{32,9... | collective-permute-start | bytes 73736 | tf_op jit(solution)/shard_map/while/body/eval_jaxpr/ppermute | solution.py:12
  (3 other events, 1.8 us)
Sparse Core Ops, SparseCore 0:
  10.1 59.1 all-gather.1
where the time goes:
time: 504 us; the launch traced here: 502 us
  waiting for transfers between devices  321 us (64%)
  starting transfers between devices  156 us (31%)
  between operations  14.1 us (3%)
  local copies, waits for them, and re-layouts  5.52 us (1%)
    ppermute x46, waiting for transfers between devices, from_behind(): return lax.ppermute(block, axis, route)  261 us
    ppermute x46, starting transfers between devices, from_behind(): return lax.ppermute(block, axis, route)  156 us
    all_gather x1, waiting for transfers between devices, on_device(): values = lax.all_gather(block_vals, 'sa', axis=2, tiled=True)[0, 0]  59 us
  transfers between devices with their start and end apart: 47, of which 25 were waited for; matrix products, arithmetic and copies ran while one was open for 1% of the time, Pallas kernels for 0%

commit v1 on v0

v1 whole, which is shorter than its diff:
```python
import functools

import jax
import jax.numpy as jnp
from jax import lax
from jax.experimental import pallas as pl
from jax.experimental.pallas import tpu as pltpu
from jax.sharding import PartitionSpec as P

MESH = pl.DeviceIdType.MESH
BLK = 128
NT = 12
NS = 6
OUTB = 32
SA = 4
OWN = OUTB // SA
N = 8


def kernel(nx, ny, source, gain, group, cols, vals, east_out, north_out, inner_out,
           weights, own_src, scaled_all, picked_src, part_send, part, traces, west, south, east, north,
           local_sem, w_send, w_recv, s_send, s_recv, p_send, p_recv, t_send, t_recv):
    gx, gy, sa = lax.axis_index("gx"), lax.axis_index("gy"), lax.axis_index("sa")
    has_west, has_east = gx > 0, gx < nx - 1
    has_south, has_north = gy > 0, gy < ny - 1
    peers = [lax.rem(sa + d, SA) for d in range(SA)]

    barrier = pltpu.get_barrier_semaphore()
    for there, dx, dy in ((has_west, -1, 0), (has_east, 1, 0), (has_south, 0, -1), (has_north, 0, 1)):
        @pl.when(there)
        def _():
            pl.semaphore_signal(barrier, inc=1, device_id=(gx + dx, gy + dy, sa), device_id_type=MESH)
    for d in range(1, SA):
        pl.semaphore_signal(barrier, inc=1, device_id=(gx, gy, peers[d]), device_id_type=MESH)

    own_rows = pl.ds(sa * OWN, OWN)
    src_load = pltpu.make_async_copy(vals.at[:, 2:4], own_src, local_sem)
    src_load.start()

    shot = lax.broadcasted_iota(jnp.int32, (N, BLK), 0)
    gains = jnp.zeros((N, BLK), jnp.float32)
    for s in range(N):
        gains = jnp.where(shot == s, gain[group[s]], gains)
    for pair in range(NS // 2):
        halves = [source[:, (2 * pair + h) * BLK:(2 * pair + h + 1) * BLK].astype(jnp.float32) * gains for h in (0, 1)]
        scaled_all[sa, pair * 16:(pair + 1) * 16, :] = jnp.concatenate(halves, axis=0).astype(jnp.bfloat16)

    neighbours = 3 + sum(there.astype(jnp.int32) for there in (has_west, has_east, has_south, has_north))
    pl.semaphore_wait(barrier, neighbours)

    def scaled_copy(owner, peer):
        return pltpu.make_async_remote_copy(scaled_all.at[owner], scaled_all.at[owner], s_send.at[peer], s_recv.at[owner],
                                            device_id=(gx, gy, peer), device_id_type=MESH)

    def weight_copy(owner, peer):
        rows = pl.ds(owner * OWN, OWN)
        return pltpu.make_async_remote_copy(vals.at[:, 0:2], weights.at[rows], w_send.at[peer], w_recv.at[owner],
                                            device_id=(gx, gy, peer), device_id_type=MESH)

    def part_copy(owner, peer):
        return pltpu.make_async_remote_copy(part_send.at[peer], part.at[owner], p_send.at[peer], p_recv.at[owner],
                                            device_id=(gx, gy, peer), device_id_type=MESH)

    for d in (2, 1, 3):
        scaled_copy(sa, peers[d]).start()
    for d in (2, 1, 3):
        weight_copy(sa, peers[d]).start()
    own_load = pltpu.make_async_copy(vals.at[:, 0:2], weights.at[own_rows], w_recv.at[sa])
    own_load.start()

    for d in (1, 3, 2):
        scaled_copy(peers[d], peers[d]).wait_recv()
    for p in range(SA):
        for pair in range(NS // 2):
            both = scaled_all[p, pair * 16:(pair + 1) * 16, :].astype(jnp.float32)
            picked_src[2 * pair, p * N:(p + 1) * N, :] = both[:N]
            picked_src[2 * pair + 1, p * N:(p + 1) * N, :] = both[N:]
    src_load.wait()
    for r in range(OWN):
        o = sa * OWN + r
        left = jnp.concatenate([picked_src[cols[o, 2]], picked_src[cols[o, 3]]], axis=1).astype(jnp.bfloat16)
        out = jnp.dot(left, own_src[r].reshape(2 * BLK, BLK), preferred_element_type=jnp.float32)
        for p in range(SA):
            part_send[p, r] = out[p * N:(p + 1) * N]
    for d in (2, 1, 3):
        part_copy(sa, peers[d]).start()
    part[sa] = part_send[sa]
    for d in (1, 3, 2):
        part_copy(peers[d], peers[d]).wait_recv()

    def trace_copy(k, src, dst, dx, dy):
        return pltpu.make_async_remote_copy(src, dst, t_send.at[k], t_recv.at[k], device_id=(gx + dx, gy + dy, sa),
                                            device_id_type=MESH)

    east_copy = trace_copy(0, east, west, 1, 0)
    north_copy = trace_copy(1, north, south, 0, 1)

    def arrived(p):
        rows = pl.ds(p * OWN, OWN)
        pltpu.make_async_copy(vals.at[:, 0:2], weights.at[rows], w_recv.at[p]).wait()

    for p in range(SA - 1):
        arrived(p)

    for there, copy, ref, base in ((has_south, north_copy, south, NS + NT), (has_west, east_copy, west, NS)):
        @pl.when(there)
        def _():
            copy.wait_recv()
            for pair in range(NT // 2):
                both = ref[pair * 16:(pair + 1) * 16, :].astype(jnp.float32)
                traces[base + 2 * pair] = both[:N]
                traces[base + 2 * pair + 1] = both[N:]

        @pl.when(jnp.logical_not(there))
        def _():
            for b in range(NT):
                traces[base + b] = jnp.zeros((N, BLK), jnp.float32)

    def row(o):
        left = jnp.concatenate([traces[cols[o, 0]], traces[cols[o, 1]]], axis=1).astype(jnp.bfloat16)
        out = jnp.dot(left, weights[o].reshape(2 * BLK, BLK), preferred_element_type=jnp.float32)
        return out + part[o // OWN, o % OWN]

    for first, ref, there, copy in ((0, east, has_east, east_copy), (NT, north, has_north, north_copy)):
        for pair in range(NT // 2):
            both = jnp.concatenate([row(first + 2 * pair), row(first + 2 * pair + 1)], axis=0)
            ref[pair * 16:(pair + 1) * 16, :] = both.astype(jnp.bfloat16)

        @pl.when(there)
        def _():
            copy.start()

    arrived(SA - 1)
    for o in range(2 * NT, OUTB):
        inner_out[:, (o - 2 * NT) * BLK:(o - 2 * NT + 1) * BLK] = row(o).astype(jnp.bfloat16)
    for ref, out in ((east, east_out), (north, north_out)):
        for pair in range(NT // 2):
            both = ref[pair * 16:(pair + 1) * 16, :]
            out[:, 2 * pair * BLK:(2 * pair + 1) * BLK] = both[:N]
            out[:, (2 * pair + 1) * BLK:(2 * pair + 2) * BLK] = both[N:]

    for d in (1, 2, 3):
        scaled_copy(sa, peers[d]).wait_send()
        weight_copy(sa, peers[d]).wait_send()
        part_copy(sa, peers[d]).wait_send()
    for there, copy in ((has_east, east_copy), (has_north, north_copy)):
        @pl.when(there)
        def _():
            copy.wait_send()


def on_device(nx, ny, source, group_gain, shot_group, block_cols, block_vals):
    vmem, smem = pl.BlockSpec(memory_space=pltpu.VMEM), pl.BlockSpec(memory_space=pltpu.SMEM)
    dma = pltpu.SemaphoreType.DMA
    bf16, f32 = jnp.bfloat16, jnp.float32
    outs = pl.pallas_call(
        functools.partial(kernel, nx, ny),
        out_shape=[jax.ShapeDtypeStruct((N, NT * BLK), bf16), jax.ShapeDtypeStruct((N, NT * BLK), bf16),
                   jax.ShapeDtypeStruct((N, (OUTB - 2 * NT) * BLK), bf16)],
        in_specs=[vmem, smem, smem, smem, pl.BlockSpec(memory_space=pl.ANY)],
        out_specs=[vmem, vmem, vmem],
        scratch_shapes=[
            pltpu.VMEM((OUTB, 2, BLK, BLK), bf16),
            pltpu.VMEM((OWN, 2, BLK, BLK), bf16),
            pltpu.VMEM((SA, NS * N, BLK), bf16),
            pltpu.VMEM((NS, SA * N, BLK), f32),
            pltpu.VMEM((SA, OWN, N, BLK), f32),
            pltpu.VMEM((SA, OWN, N, BLK), f32),
            pltpu.VMEM((NS + 2 * NT, N, BLK), f32),
            pltpu.VMEM((NT * N, BLK), bf16),
            pltpu.VMEM((NT * N, BLK), bf16),
            pltpu.VMEM((NT * N, BLK), bf16),
            pltpu.VMEM((NT * N, BLK), bf16),
            dma, dma((SA,)), dma((SA,)), dma((SA,)), dma((SA,)), dma((SA,)), dma((SA,)), dma((2,)), dma((2,)),
        ],
        compiler_params=pltpu.CompilerParams(collective_id=0, has_side_effects=True, vmem_limit_bytes=40 << 20),
        name="sweep",
    )(source[0, 0], group_gain, shot_group, block_cols[0, 0], block_vals[0, 0])
    return tuple(out[None, None] for out in outs)


def solution(mesh):
    placed = (
        P("gx", "gy", "sa", None),
        P(),
        P("sa"),
        P("gx", "gy", None, None),
        P("gx", "gy", "sa", None, None, None),
    )
    return jax.shard_map(
        functools.partial(on_device, mesh.shape["gx"], mesh.shape["gy"]),
        mesh=mesh,
        in_specs=placed,
        out_specs=(P("gx", "gy", "sa", None), P("gx", "gy", "sa", None), P("gx", "gy", "sa", None)),
        check_vma=False,
    )
```

time: 504 us -> 125 us (0.25)
  the two profiles are of different devices: /device:TPU:105 before, /device:TPU:505 now
where the time goes in v1:
time: 125 us
  Pallas kernels  121 us (97%)
  local copies, waits for them, and re-layouts  3.84 us (3%)
    pallas_call x1, Pallas kernels, on_device(): pl.pallas_call(functools.partial(kernel, nx, ny), out_shape=[jax.ShapeDty...  121 us
    unnamed x11, local copies, waits for them, and re-layouts  3.06 us

profile of v1, /device:TPU:505, one launch (start us, length us, event | category | flops | bytes accessed | tf_op | source)
XLA Modules:
  0.0 125.1 jit_solution(2966840452715248278)
XLA Ops:
  0.6 0.0 copy-start.1
  0.6 0.0 copy-start.2
  0.7 0.0 copy-start.3
  0.7 0.8 copy.8.cols
  1.4 0.0 copy-done.1
  1.4 0.0 copy-done.2
  1.4 0.0 copy-done.3
  1.5 0.0 copy-start
  1.5 1.2 copy-done
  2.7 120.6 %sweep.1 = (bf16[8,1536]{1,0:T(8,128)(2,1)S(1)}, bf16[8,1536]{1,0:T(8,128)(2,1)S(1)}, bf16[8,1024]{1,0:T(8,128)(2,1)S(1)}) custom-call(bf16[8,768]{1,0:T(8,128)(2,1)S(1)} %bitcast.10, f32[4]{0:T(128)S(1)} %copy-done.2, s32[8]{0:T(128)S(1)} %copy-done.3, s32[32,4]{1,0:T(8,128)S(1)} %copy.8.cols, bf16[8,4,128,128]{3,2,1,0:T(8,128)(2,1)S(1)} %bitcast.6), custom_call_target="tpu_custom_call" | custom-call | tf_op jit(solution)/shard_map/sweep/pallas_call | solution.py:156
  123.3 0.6 copy.12
  123.9 0.6 copy.13
  124.5 0.6 copy.14
Async XLA Ops:
  0.6 0.8 copy-start.1
  0.6 0.8 copy-start.2
  0.7 0.8 copy-start.3
  1.5 1.2 copy-start

commit v2 on v1

--- a/solution.py
+++ b/solution.py
@@ -17,7 +17,7 @@
 N = 8
 
 
-def kernel(nx, ny, source, gain, group, cols, vals, east_out, north_out, inner_out,
+def kernel(nx, ny, source, gain, group, cols, vals, outs,
            weights, own_src, scaled_all, picked_src, part_send, part, traces, west, south, east, north,
            local_sem, w_send, w_recv, s_send, s_recv, p_send, p_recv, t_send, t_recv):
     gx, gy, sa = lax.axis_index("gx"), lax.axis_index("gy"), lax.axis_index("sa")
@@ -33,7 +33,6 @@
     for d in range(1, SA):
         pl.semaphore_signal(barrier, inc=1, device_id=(gx, gy, peers[d]), device_id_type=MESH)
 
-    own_rows = pl.ds(sa * OWN, OWN)
     src_load = pltpu.make_async_copy(vals.at[:, 2:4], own_src, local_sem)
     src_load.start()
 
@@ -52,10 +51,29 @@
         return pltpu.make_async_remote_copy(scaled_all.at[owner], scaled_all.at[owner], s_send.at[peer], s_recv.at[owner],
                                             device_id=(gx, gy, peer), device_id_type=MESH)
 
-    def weight_copy(owner, peer):
+    def weight_copy(k, owner, peer):
         rows = pl.ds(owner * OWN, OWN)
-        return pltpu.make_async_remote_copy(vals.at[:, 0:2], weights.at[rows], w_send.at[peer], w_recv.at[owner],
-                                            device_id=(gx, gy, peer), device_id_type=MESH)
+        return pltpu.make_async_remote_copy(vals.at[:, k:k + 1], weights.at[rows, k:k + 1], w_send.at[k, peer],
+                                            w_recv.at[k, owner], device_id=(gx, gy, peer), device_id_type=MESH)
+
+    def own_copy(k, p):
+        rows = pl.ds(p * OWN, OWN)
+        return pltpu.make_async_copy(vals.at[:, k:k + 1], weights.at[rows, k:k + 1], w_recv.at[k, p])
+
+    needed = (has_west, has_south)
+
+    def send_weights():
+        for k in (1, 0):
+            @pl.when(needed[k])
+            def _():
+                for d in (2, 1, 3):
+                    weight_copy(k, sa, peers[d]).start()
+
+    def arrived(p):
+        for k in (1, 0):
+            @pl.when(needed[k])
+            def _():
+                own_copy(k, p).wait()
 
     def part_copy(owner, peer):
         return pltpu.make_async_remote_copy(part_send.at[peer], part.at[owner], p_send.at[peer], p_recv.at[owner],
@@ -63,10 +81,6 @@
 
     for d in (2, 1, 3):
         scaled_copy(sa, peers[d]).start()
-    for d in (2, 1, 3):
-        weight_copy(sa, peers[d]).start()
-    own_load = pltpu.make_async_copy(vals.at[:, 0:2], weights.at[own_rows], w_recv.at[sa])
-    own_load.start()
 
     for d in (1, 3, 2):
         scaled_copy(peers[d], peers[d]).wait_recv()
@@ -78,12 +92,21 @@
     src_load.wait()
     for r in range(OWN):
         o = sa * OWN + r
-        left = jnp.concatenate([picked_src[cols[o, 2]], picked_src[cols[o, 3]]], axis=1).astype(jnp.bfloat16)
+        left = jnp.concatenate([picked_src[cols[2, o]], picked_src[cols[3, o]]], axis=1).astype(jnp.bfloat16)
         out = jnp.dot(left, own_src[r].reshape(2 * BLK, BLK), preferred_element_type=jnp.float32)
         for p in range(SA):
             part_send[p, r] = out[p * N:(p + 1) * N]
     for d in (2, 1, 3):
         part_copy(sa, peers[d]).start()
+    pl.when(sa < SA - 1)(send_weights)
+    for k in (1, 0):
+        @pl.when(needed[k])
+        def _():
+            own_copy(k, sa).start()
+
+        @pl.when(jnp.logical_not(needed[k]))
+        def _():
+            weights[:, k] = jnp.zeros((OUTB, BLK, BLK), jnp.bfloat16)
     part[sa] = part_send[sa]
     for d in (1, 3, 2):
         part_copy(peers[d], peers[d]).wait_recv()
@@ -95,12 +118,9 @@
     east_copy = trace_copy(0, east, west, 1, 0)
     north_copy = trace_copy(1, north, south, 0, 1)
 
-    def arrived(p):
-        rows = pl.ds(p * OWN, OWN)
-        pltpu.make_async_copy(vals.at[:, 0:2], weights.at[rows], w_recv.at[p]).wait()
-
     for p in range(SA - 1):
         arrived(p)
+    pl.when(sa == SA - 1)(send_weights)
 
     for there, copy, ref, base in ((has_south, north_copy, south, NS + NT), (has_west, east_copy, west, NS)):
         @pl.when(there)
@@ -117,7 +137,7 @@
                 traces[base + b] = jnp.zeros((N, BLK), jnp.float32)
 
     def row(o):
-        left = jnp.concatenate([traces[cols[o, 0]], traces[cols[o, 1]]], axis=1).astype(jnp.bfloat16)
+        left = jnp.concatenate([traces[cols[0, o]], traces[cols[1, o]]], axis=1).astype(jnp.bfloat16)
         out = jnp.dot(left, weights[o].reshape(2 * BLK, BLK), preferred_element_type=jnp.float32)
         return out + part[o // OWN, o % OWN]
 
@@ -132,16 +152,19 @@
 
     arrived(SA - 1)
     for o in range(2 * NT, OUTB):
-        inner_out[:, (o - 2 * NT) * BLK:(o - 2 * NT + 1) * BLK] = row(o).astype(jnp.bfloat16)
-    for ref, out in ((east, east_out), (north, north_out)):
+        outs[:, o * BLK:(o + 1) * BLK] = row(o).astype(jnp.bfloat16)
+    for ref, base in ((east, 0), (north, NT)):
         for pair in range(NT // 2):
             both = ref[pair * 16:(pair + 1) * 16, :]
-            out[:, 2 * pair * BLK:(2 * pair + 1) * BLK] = both[:N]
-            out[:, (2 * pair + 1) * BLK:(2 * pair + 2) * BLK] = both[N:]
+            outs[:, (base + 2 * pair) * BLK:(base + 2 * pair + 1) * BLK] = both[:N]
+            outs[:, (base + 2 * pair + 1) * BLK:(base + 2 * pair + 2) * BLK] = both[N:]
 
     for d in (1, 2, 3):
         scaled_copy(sa, peers[d]).wait_send()
-        weight_copy(sa, peers[d]).wait_send()
+        for k in (0, 1):
+            @pl.when(needed[k])
+            def _():
+                weight_copy(k, sa, peers[d]).wait_send()
         part_copy(sa, peers[d]).wait_send()
     for there, copy in ((has_east, east_copy), (has_north, north_copy)):
         @pl.when(there)
@@ -155,10 +178,9 @@
     bf16, f32 = jnp.bfloat16, jnp.float32
     outs = pl.pallas_call(
         functools.partial(kernel, nx, ny),
-        out_shape=[jax.ShapeDtypeStruct((N, NT * BLK), bf16), jax.ShapeDtypeStruct((N, NT * BLK), bf16),
-                   jax.ShapeDtypeStruct((N, (OUTB - 2 * NT) * BLK), bf16)],
+        out_shape=jax.ShapeDtypeStruct((N, OUTB * BLK), bf16),
         in_specs=[vmem, smem, smem, smem, pl.BlockSpec(memory_space=pl.ANY)],
-        out_specs=[vmem, vmem, vmem],
+        out_specs=vmem,
         scratch_shapes=[
             pltpu.VMEM((OUTB, 2, BLK, BLK), bf16),
             pltpu.VMEM((OWN, 2, BLK, BLK), bf16),
@@ -171,12 +193,13 @@
             pltpu.VMEM((NT * N, BLK), bf16),
             pltpu.VMEM((NT * N, BLK), bf16),
             pltpu.VMEM((NT * N, BLK), bf16),
-            dma, dma((SA,)), dma((SA,)), dma((SA,)), dma((SA,)), dma((SA,)), dma((SA,)), dma((2,)), dma((2,)),
+            dma, dma((2, SA)), dma((2, SA)), dma((SA,)), dma((SA,)), dma((SA,)), dma((SA,)), dma((2,)), dma((2,)),
         ],
-        compiler_params=pltpu.CompilerParams(collective_id=0, has_side_effects=True, vmem_limit_bytes=40 << 20),
+        compiler_params=pltpu.CompilerParams(collective_id=0, has_side_effects=True, vmem_limit_bytes=63 << 20),
         name="sweep",
-    )(source[0, 0], group_gain, shot_group, block_cols[0, 0], block_vals[0, 0])
-    return tuple(out[None, None] for out in outs)
+    )(source[0, 0], group_gain, shot_group, block_cols[0, 0].T, block_vals[0, 0])
+    outs = outs[None, None]
+    return outs[..., :NT * BLK], outs[..., NT * BLK:2 * NT * BLK], outs[..., 2 * NT * BLK:]
 
 
 def solution(mesh):

time: 125 us -> 111 us (0.89)
  Pallas kernels: 121 us -> 107 us
    pallas_call x1, Pallas kernels: 121 us -> 107 us  [on_device(): pl.pallas_call(functools.partial(kernel, nx, ny), out_shape=jax.ShapeDtyp...]
    unnamed x11 -> x0, local copies, waits for them, and re-layouts: 3.06 us -> none
    slice x0 -> x2, local copies, waits for them, and re-layouts: none -> 2.7 us  [the longest x1 1.38 us: on_device(): outs[..., NT * BLK:2 * NT * BLK]]
where the time goes in v2:
time: 111 us
  Pallas kernels  107 us (96%)
  local copies, waits for them, and re-layouts  2.7 us (2%)
    pallas_call x1, Pallas kernels, on_device(): pl.pallas_call(functools.partial(kernel, nx, ny), out_shape=jax.ShapeDtyp...  107 us

profile of v2, /device:TPU:505, one launch (start us, length us, event | category | flops | bytes accessed | tf_op | source)
XLA Modules:
  0.0 110.6 jit_solution(11193571296030650209)
XLA Ops:
  0.6 107.3 %sweep.1 = bf16[8,4096]{1,0:T(8,128)(2,1)} custom-call(bf16[8,768]{1,0:T(8,128)(2,1)} %bitcast.9, f32[4]{0:T(128)} %gain.1, s32[8]{0:T(128)} %group.1, s32[4,32]{1,0:T(4,128)} %bitcast.10, bf16[8,4,128,128]{3,2,1,0:T(8,128)(2,1)} %bitcast.6), custom_call_target="tpu_custom_call" | custom-call | tf_op jit(solution)/shard_map/sweep/pallas_call | solution.py:179
  107.9 1.4 %fusion = (bf16[1,1,8,1536]{3,2,1,0:T(8,128)(2,1)}, bf16[1,1,8,1536]{3,2,1,0:T(8,128)(2,1)}) fusion(bf16[1,1,8,4096]{3,2,1,0:T(8,128)(2,1)} %bitcast.7), kind=kLoop, calls=%fused_computation | loop fusion | bytes 98304 | tf_op jit(solution)/shard_map/slice | solution.py:202
  109.3 1.3 %slice.14 = bf16[1,1,8,1024]{3,2,1,0:T(8,128)(2,1)} slice(bf16[1,1,8,4096]{3,2,1,0:T(8,128)(2,1)} %bitcast.8), slice={[0:1], [0:1], [0:8], [3072:4096]} | slice | bytes 32768 | tf_op jit(solution)/shard_map/slice | solution.py:202

commit v3 on v2

v3 whole, which is shorter than its diff:
```python
import functools

import jax
import jax.numpy as jnp
from jax import lax
from jax.experimental import pallas as pl
from jax.experimental.pallas import tpu as pltpu
from jax.sharding import PartitionSpec as P

MESH = pl.DeviceIdType.MESH
BLK = 128
NT = 12
NS = 6
OUTB = 32
SA = 4
OWN = OUTB // SA
N = 8
TRACED = 2 * NT
SENT = TRACED // SA


def sent_slot(o):
    owner, r = divmod(o, OWN)
    return (owner, r) if r < SENT else (SA - 1, (OWN - SENT) * owner + r - SENT)


def kernel(nx, ny, source, gain, group, cols, cols_hbm, vals, east_out, north_out, inner_out,
           weights, own_src, scaled_all, picked_src, part_send, part, traces, west, south, east, north,
           moved, stage, part_moved, part_e, cols_vmem, cols_e, traces_e, west_e, south_e, east_e, north_e,
           local_sem, w_send, w_recv, s_send, s_recv, p_send, p_recv, t_send, t_recv,
           h_send, h_recv, z_send, e_recv, m_send, m_recv, go_sem):
    gx, gy, sa = lax.axis_index("gx"), lax.axis_index("gy"), lax.axis_index("sa")
    odd = lax.rem(gx, 2)
    z = gy // 2
    peers = [lax.rem(sa + d, SA) for d in range(SA)]
    donor = (odd == 0) & (gx > 1)
    host = (odd == 1) & (gx > 1)
    works = jnp.logical_not(donor)
    has_west, has_south, has_north = gx > 0, gy > 0, gy < ny - 1
    z_odd = lax.rem(z, 2) == 1
    chained = donor & z_odd

    barrier = pltpu.get_barrier_semaphore()
    contacts = (
        (odd == 0, 1, 0), (odd == 1, -1, 0), ((odd == 1) & (gx < nx - 1), 2, 0), (host, -2, 0),
        (works & has_south, 0, -1), (works & has_north, 0, 1),
        (chained & (gy >= 4), 0, -4), (chained & (gy < ny - 4), 0, 4),
    )
    for there, dx, dy in contacts:
        @pl.when(there)
        def _():
            pl.semaphore_signal(barrier, inc=1, device_id=(gx + dx, gy + dy, sa), device_id_type=MESH)
    for d in range(1, SA):
        pl.semaphore_signal(barrier, inc=1, device_id=(gx, gy, peers[d]), device_id_type=MESH)

    src_load = pltpu.make_async_copy(vals.at[:, 2:4], own_src, local_sem)
    src_load.start()

    shot = lax.broadcasted_iota(jnp.int32, (N, BLK), 0)
    gains = jnp.zeros((N, BLK), jnp.float32)
    for s in range(N):
        gains = jnp.where(shot == s, gain[group[s]], gains)
    for pair in range(NS // 2):
        halves = [source[:, (2 * pair + h) * BLK:(2 * pair + h + 1) * BLK].astype(jnp.float32) * gains for h in (0, 1)]
        scaled_all[sa, pair * 16:(pair + 1) * 16, :] = jnp.concatenate(halves, axis=0).astype(jnp.bfloat16)

    pl.semaphore_wait(barrier, 3 + sum(there.astype(jnp.int32) for there, _, _ in contacts))

    def copy(src, dst, send, recv, dx=0, dy=0, to=None):
        return pltpu.make_async_remote_copy(src, dst, send, recv, device_id=(gx + dx, gy + dy, sa if to is None else to),
                                            device_id_type=MESH)

    def scaled_copy(owner, peer):
        return copy(scaled_all.at[owner], scaled_all.at[owner], s_send.at[peer], s_recv.at[owner], to=peer)

    def part_copy(owner, peer):
        return copy(part_send.at[peer], part.at[owner], p_send.at[peer], p_recv.at[owner], to=peer)

    def weight_copy(k, owner, peer):
        rows = pl.ds(owner * OWN, OWN)
        return copy(vals.at[:, k:k + 1], weights.at[rows, k:k + 1], w_send.at[k, peer], w_recv.at[k, owner], to=peer)

    def own_copy(k, p):
        rows = pl.ds(p * OWN, OWN)
        return pltpu.make_async_copy(vals.at[:, k:k + 1], weights.at[rows, k:k + 1], w_recv.at[k, p])

    needed = (has_west, has_south)

    def send_weights():
        for k in (1, 0):
            @pl.when(needed[k])
            def _():
                for d in (2, 1, 3):
                    weight_copy(k, sa, peers[d]).start()

    def arrived(p):
        for k in (1, 0):
            @pl.when(needed[k])
            def _():
                own_copy(k, p).wait()

    def shuffle_copy(owner):
        lot = OWN - SENT
        return copy(vals.at[pl.ds(SENT, lot), 0:2], stage.at[pl.ds(owner * lot, lot)], h_send, h_recv.at[owner], to=SA - 1)

    def move_copy(k, last):
        src = stage.at[:, k] if last else vals.at[pl.ds(0, SENT), k]
        return copy(src, moved.at[sa, k], z_send.at[k], m_recv.at[k, sa], dx=1)

    def moved_copy(k, owner, peer):
        return copy(moved.at[owner, k], moved.at[owner, k], m_send.at[k, peer], m_recv.at[k, owner], to=peer)

    part_move = copy(part_moved, part_e, z_send.at[2], e_recv.at[0], dx=1)
    cols_move = copy(cols_hbm, cols_vmem, z_send.at[3], e_recv.at[1], dx=1)

    def moves(act):
        @pl.when(sa < SA - 1)
        def _():
            act(move_copy(0, False))
            pl.when(has_south)(lambda: act(move_copy(1, False)))

        @pl.when(sa == SA - 1)
        def _():
            act(move_copy(0, True))
            pl.when(has_south)(lambda: act(move_copy(1, True)))

    def start_moves():
        @pl.when(sa == SA - 1)
        def _():
            for owner in range(SA - 1):
                shuffle_copy(owner).wait_recv()
        moves(lambda c: c.start())

    for d in (2, 1, 3):
        scaled_copy(sa, peers[d]).start()

    @pl.when(donor)
    def _():
        cols_move.start()
        pl.when(sa < SA - 1)(lambda: shuffle_copy(sa).start())
    early = donor & (jnp.logical_not(z_odd) | (z == 1))
    late = donor & z_odd & (z > 1)
    pl.when(early & (sa < SA - 1))(start_moves)

    for d in (1, 3, 2):
        scaled_copy(peers[d], peers[d]).wait_recv()
    for p in range(SA):
        for pair in range(NS // 2):
            both = scaled_all[p, pair * 16:(pair + 1) * 16, :].astype(jnp.float32)
            picked_src[2 * pair, p * N:(p + 1) * N, :] = both[:N]
            picked_src[2 * pair + 1, p * N:(p + 1) * N, :] = both[N:]
    src_load.wait()
    for r in range(OWN):
        o = sa * OWN + r
        left = jnp.concatenate([picked_src[cols[2, o]], picked_src[cols[3, o]]], axis=1).astype(jnp.bfloat16)
        out = jnp.dot(left, own_src[r].reshape(2 * BLK, BLK), preferred_element_type=jnp.float32)
        for p in range(SA):
            part_send[p, r] = out[p * N:(p + 1) * N]
    for d in (2, 1, 3):
        part_copy(sa, peers[d]).start()
    pl.when(early & (sa == SA - 1))(start_moves)

    pl.when(works & (sa < SA - 1))(send_weights)
    gathers = works | (sa == SA - 1)
    for k in (1, 0):
        @pl.when(needed[k] & gathers)
        def _():
            own_copy(k, sa).start()

        @pl.when(jnp.logical_not(needed[k]))
        def _():
            weights[:, k] = jnp.zeros((OUTB, BLK, BLK), jnp.bfloat16)
    part[sa] = part_send[sa]
    for d in (1, 3, 2):
        part_copy(peers[d], peers[d]).wait_recv()

    def unpack(ref, dst, base):
        for pair in range(NT // 2):
            both = ref[pair * 16:(pair + 1) * 16, :].astype(jnp.float32)
            dst[base + 2 * pair] = both[:N]
            dst[base + 2 * pair + 1] = both[N:]

    def clear(dst, base):
        for b in range(NT):
            dst[base + b] = jnp.zeros((N, BLK), jnp.float32)

    def row(o):
        left = jnp.concatenate([traces[cols[0, o]], traces[cols[1, o]]], axis=1).astype(jnp.bfloat16)
        out = jnp.dot(left, weights[o].reshape(2 * BLK, BLK), preferred_element_type=jnp.float32)
        return out + part[o // OWN, o % OWN]

    def row_e(o):
        left = jnp.concatenate([traces_e[cols_e[0, o]], traces_e[cols_e[1, o]]], axis=1).astype(jnp.bfloat16)
        p, r = sent_slot(o)
        blocks = jnp.concatenate([moved[p, 0, r], moved[p, 1, r]], axis=0)
        return jnp.dot(left, blocks, preferred_element_type=jnp.float32)

    def interior():
        for o in range(TRACED, OUTB):
            inner_out[:, (o - TRACED) * BLK:(o - TRACED + 1) * BLK] = row(o).astype(jnp.bfloat16)

    def put_out():
        for ref, out in ((east, east_out), (north, north_out)):
            for pair in range(NT // 2):
                both = ref[pair * 16:(pair + 1) * 16, :]
                out[:, 2 * pair * BLK:(2 * pair + 1) * BLK] = both[:N]
                out[:, (2 * pair + 1) * BLK:(2 * pair + 2) * BLK] = both[N:]

    west_copy = copy(east, west, t_send.at[0], t_recv.at[0], dx=1)
    west_e_copy = copy(east, west_e, t_send.at[0], t_recv.at[2], dx=2)
    south_copy = copy(north, south, t_send.at[1], t_recv.at[1], dy=1)
    south_e_copy = copy(north_e, south_e, t_send.at[2], t_recv.at[3], dy=1)
    back_west = copy(west_e, west, t_send.at[3], t_recv.at[0], dx=-1)
    back_south = copy(south_e, south, t_send.at[4], t_recv.at[1], dx=-1)
    back_east = copy(east_e, east, t_send.at[5], t_recv.at[4], dx=-1)
    back_north = copy(north_e, north, t_send.at[6], t_recv.at[5], dx=-1)

    @pl.when(donor)
    def _():
        for o in range(0, TRACED, 2):
            both = jnp.concatenate([part[o // OWN, o % OWN], part[o // OWN, o % OWN + 1]], axis=0)
            part_moved[o * N:(o + 2) * N, :] = both.astype(jnp.bfloat16)

        @pl.when(late)
        def _():
            pl.semaphore_wait(go_sem, 1)
            start_moves()
        part_move.start()
        moves(lambda c: c.wait_send())
        part_move.wait_send()

        @pl.when(chained & (gy < ny - 4))
        def _():
            pl.semaphore_signal(go_sem, inc=1, device_id=(gx, gy + 4, sa), device_id_type=MESH)
        pl.when(sa == SA - 1)(send_weights)
        arrived(SA - 1)
        back_west.wait_recv()
        unpack(west, traces, NS)

        @pl.when(has_south)
        def _():
            back_south.wait_recv()
            unpack(south, traces, NS + NT)
        pl.when(jnp.logical_not(has_south))(lambda: clear(traces, NS + NT))
        interior()
        back_east.wait_recv()
        back_north.wait_recv()
        put_out()
        cols_move.wait_send()
        pl.when(sa < SA - 1)(lambda: shuffle_copy(sa).wait_send())

        @pl.when(sa == SA - 1)
        def _():
            for k in (0, 1):
                @pl.when(needed[k])
                def _():
                    for d in (1, 2, 3):
                        weight_copy(k, sa, peers[d]).wait_send()

    @pl.when(host)
    def _():
        @pl.when(jnp.logical_not(has_south))
        def _():
            for p in range(SA):
                moved[p, 1] = jnp.zeros((SENT, BLK, BLK), jnp.bfloat16)
        for k in (0, 1):
            @pl.when(needed[k])
            def _():
                moved_copy(k, sa, peers[1]).wait_recv()
                for d in (2, 1, 3):
                    moved_copy(k, sa, peers[d]).start()

    @pl.when(works)
    def _():
        for p in range(SA - 1):
            arrived(p)
        pl.when(sa == SA - 1)(send_weights)

    @pl.when(host)
    def _():
        cols_move.wait_recv()
        to_smem = pltpu.make_async_copy(cols_vmem, cols_e, local_sem)
        to_smem.start()
        to_smem.wait()
        part_move.wait_recv()
        for k in (0, 1):
            @pl.when(needed[k])
            def _():
                for d in (1, 3, 2):
                    moved_copy(k, peers[d], sa).wait_recv()

        @pl.when(has_south)
        def _():
            south_e_copy.wait_recv()
            unpack(south_e, traces_e, NS + NT)
        pl.when(jnp.logical_not(has_south))(lambda: clear(traces_e, NS + NT))
        west_e_copy.wait_recv()
        unpack(west_e, traces_e, NS)
        for base, ref in ((NT, north_e), (0, east_e)):
            for o in range(base, base + NT, 2):
                both = jnp.concatenate([row_e(o), row_e(o + 1)], axis=0)
                both = (both + part_e[o * N:(o + 2) * N, :].astype(jnp.float32)).astype(jnp.bfloat16)
                ref[(o - base) * N:(o - base + 2) * N, :] = both
            if base:
                pl.when(has_north)(lambda: south_e_copy.start())
        unpack(east_e, traces, NS)

    @pl.when(works)
    def _():
        @pl.when(gx == 1)
        def _():
            west_copy.wait_recv()
            unpack(west, traces, NS)
        pl.when(gx == 0)(lambda: clear(traces, NS))

        @pl.when(has_south)
        def _():
            south_copy.wait_recv()
            unpack(south, traces, NS + NT)
        pl.when(jnp.logical_not(has_south))(lambda: clear(traces, NS + NT))
        for base, ref in ((0, east), (NT, north)):
            for o in range(base, base + NT, 2):
                both = jnp.concatenate([row(o), row(o + 1)], axis=0)
                ref[(o - base) * N:(o - base + 2) * N, :] = both.astype(jnp.bfloat16)
            if base:
                pl.when(has_north)(lambda: south_copy.start())
            else:
                pl.when(gx == 0)(lambda: west_copy.start())
                pl.when((odd == 1) & (gx < nx - 1))(lambda: west_e_copy.start())

        @pl.when(host)
        def _():
            back_west.start()
            pl.when(has_south)(lambda: back_south.start())
            back_east.start()
            back_north.start()
        arrived(SA - 1)
        interior()
        put_out()
        for d in (1, 2, 3):
            for k in (0, 1):
                @pl.when(needed[k])
                def _():
                    weight_copy(k, sa, peers[d]).wait_send()
        pl.when(has_north)(lambda: south_copy.wait_send())
        pl.when(gx == 0)(lambda: west_copy.wait_send())
        pl.when((odd == 1) & (gx < nx - 1))(lambda: west_e_copy.wait_send())

        @pl.when(host)
        def _():
            for k in (0, 1):
                @pl.when(needed[k])
                def _():
                    for d in (1, 2, 3):
                        moved_copy(k, sa, peers[d]).wait_send()
            pl.when(has_north)(lambda: south_e_copy.wait_send())
            back_west.wait_send()
            pl.when(has_south)(lambda: back_south.wait_send())
            back_east.wait_send()
            back_north.wait_send()

    for d in (1, 2, 3):
        scaled_copy(sa, peers[d]).wait_send()
        part_copy(sa, peers[d]).wait_send()


def on_device(nx, ny, source, group_gain, shot_group, block_cols, block_vals):
    vmem, smem, hbm = (pl.BlockSpec(memory_space=m) for m in (pltpu.VMEM, pltpu.SMEM, pl.ANY))
    dma = pltpu.SemaphoreType.DMA
    bf16, f32 = jnp.bfloat16, jnp.float32
    trace = pltpu.VMEM((NT * N, BLK), bf16)
    cols = block_cols[0, 0].T
    outs = pl.pallas_call(
        functools.partial(kernel, nx, ny),
        out_shape=[jax.ShapeDtypeStruct((N, NT * BLK), bf16), jax.ShapeDtypeStruct((N, NT * BLK), bf16),
                   jax.ShapeDtypeStruct((N, (OUTB - TRACED) * BLK), bf16)],
        in_specs=[vmem, smem, smem, smem, hbm, hbm],
        out_specs=[vmem, vmem, vmem],
        scratch_shapes=[
            pltpu.VMEM((OUTB, 2, BLK, BLK), bf16),
            pltpu.VMEM((OWN, 2, BLK, BLK), bf16),
            pltpu.VMEM((SA, NS * N, BLK), bf16),
            pltpu.VMEM((NS, SA * N, BLK), f32),
            pltpu.VMEM((SA, OWN, N, BLK), f32),
            pltpu.VMEM((SA, OWN, N, BLK), f32),
            pltpu.VMEM((NS + 2 * NT, N, BLK), f32),
            trace, trace, trace, trace,
            pltpu.VMEM((SA, 2, SENT, BLK, BLK), bf16),
            pltpu.VMEM((SENT, 2, BLK, BLK), bf16),
            pltpu.VMEM((TRACED * N, BLK), bf16),
            pltpu.VMEM((TRACED * N, BLK), bf16),
            pltpu.VMEM(cols.shape, jnp.int32),
            pltpu.SMEM(cols.shape, jnp.int32),
            pltpu.VMEM((NS + 2 * NT, N, BLK), f32),
            trace, trace, trace, trace,
            dma, dma((2, SA)), dma((2, SA)), dma((SA,)), dma((SA,)), dma((SA,)), dma((SA,)), dma((7,)), dma((6,)),
            dma, dma((SA - 1,)), dma((4,)), dma((2,)), dma((2, SA)), dma((2, SA)), pltpu.SemaphoreType.REGULAR,
        ],
        compiler_params=pltpu.CompilerParams(collective_id=0, has_side_effects=True, vmem_limit_bytes=63 << 20),
        name="sweep",
    )(source[0, 0], group_gain, shot_group, cols, cols, block_vals[0, 0])
    return tuple(out[None, None] for out in outs)


def solution(mesh):
    placed = (
        P("gx", "gy", "sa", None),
        P(),
        P("sa"),
        P("gx", "gy", None, None),
        P("gx", "gy", "sa", None, None, None),
    )
    return jax.shard_map(
        functools.partial(on_device, mesh.shape["gx"], mesh.shape["gy"]),
        mesh=mesh,
        in_specs=placed,
        out_specs=(P("gx", "gy", "sa", None), P("gx", "gy", "sa", None), P("gx", "gy", "sa", None)),
        check_vma=False,
    )
```

time: 111 us -> 102 us (0.919)
  the two profiles are of different devices: /device:TPU:505 before, /device:TPU:255 now
where the time goes in v3:
time: 102 us
  Pallas kernels  98.4 us (96%)
  local copies, waits for them, and re-layouts  2.69 us (3%)
    pallas_call x1, Pallas kernels, on_device(): pl.pallas_call(functools.partial(kernel, nx, ny), out_shape=[jax.ShapeDty...  98.4 us
    unnamed x7, local copies, waits for them, and re-layouts  2.69 us

profile of v3, /device:TPU:255, one launch (start us, length us, event | category | flops | bytes accessed | tf_op | source)
XLA Modules:
  0.0 101.7 jit_solution(15110387883258475777)
XLA Ops:
  0.6 98.4 %sweep.1 = (bf16[8,1536]{1,0:T(8,128)(2,1)}, bf16[8,1536]{1,0:T(8,128)(2,1)}, bf16[8,1024]{1,0:T(8,128)(2,1)}) custom-call(bf16[8,768]{1,0:T(8,128)(2,1)} %bitcast.12, f32[4]{0:T(128)} %gain.1, s32[8]{0:T(128)} %group.1, s32[4,32]{1,0:T(4,128)} %bitcast.13, s32[4,32]{1,0:T(4,128)} %bitcast.14, bf16[8,4,128,128]{3,2,1,0:T(8,128)(2,1)} %bitcast.8), custom_call_target="tpu_custom_call" | custom-call | tf_op jit(solution)/shard_map/sweep/pallas_call | solution.py:373
  99.0 0.0 copy-start
  99.0 1.4 %copy.11 = bf16[1,1,8,1536]{3,2,1,0:T(8,128)(2,1)} copy(bf16[1,1,8,1536]{3,2,1,0:T(8,128)(2,1)} %bitcast.10) | data formatting | bytes 49152
  100.4 0.0 copy-done
  100.4 0.0 copy-start.1
  100.4 0.6 copy.12
  101.0 0.1 copy-done.1
  101.1 0.6 copy.13
Async XLA Ops:
  99.0 1.4 %copy-start = (bf16[8,1536]{1,0:T(8,128)(2,1)S(1)}, bf16[8,1536]{1,0:T(8,128)(2,1)}, u32[]{:S(2)}) copy-start(bf16[8,1536]{1,0:T(8,128)(2,1)} %get-tuple-element.7) | copy-start | bytes 73732
  100.4 0.7 copy-start.1

commit v4 on v3

v4 whole, which is shorter than its diff:
```python
import functools

import jax
import jax.numpy as jnp
from jax import lax
from jax.experimental import pallas as pl
from jax.experimental.pallas import tpu as pltpu
from jax.sharding import PartitionSpec as P

MESH = pl.DeviceIdType.MESH
BLK = 128
NT = 12
NS = 6
OUTB = 32
SA = 4
OWN = OUTB // SA
N = 8
TRACED = 2 * NT
SENT = TRACED // SA

HALF = SENT // 2
CHUNKS = ((0, 0), (0, 1), (1, 0), (1, 1))


def sent_slot(o):
    owner, r = divmod(o, OWN)
    return (owner, r) if r < SENT else (SA - 1, (OWN - SENT) * owner + r - SENT)


def kernel(nx, ny, source, gain, group, cols, cols_hbm, vals_hbm, east_out, north_out, inner_out,
           weights, vals, scaled_all, picked_src, part_send, part, traces, west, south, east, north,
           moved, stage, part_moved, part_m, cols_vmem, cols_m, traces_m, south_m, east_m, north_m,
           local_sem, w_send, w_recv, s_send, s_recv, p_send, p_recv, t_send, t_recv,
           h_send, h_recv, z_send, z_more, e_recv, m_send, m_recv, go_sem, ack_sem):
    gx, gy, sa = lax.axis_index("gx"), lax.axis_index("gy"), lax.axis_index("sa")
    odd = lax.rem(gx, 2)
    z = gy // 2
    peers = [lax.rem(sa + d, SA) for d in range(SA)]
    donor = (odd == 1) & (gx < nx - 1)
    host = (odd == 0) & (gx < nx - 2)
    works = jnp.logical_not(donor)
    ends = gx == nx - 1
    before_end = gx == nx - 2
    has_west, has_south, has_north = gx > 0, gy > 0, gy < ny - 1
    z_odd = lax.rem(z, 2) == 1
    chained = donor & z_odd
    chains = chained & (gy < ny - 4)

    barrier = pltpu.get_barrier_semaphore()
    near = (
        ((odd == 0) & (gx < nx - 2), 2, 0), ((odd == 0) & (gx > 1), -2, 0),
        (works & has_south, 0, -1), (works & has_north, 0, 1),
        (chained & (gy >= 4), 0, -4), (chains, 0, 4),
    )
    for there, dx, dy in ((odd == 0, 1, 0),) + near:
        @pl.when(there)
        def _():
            pl.semaphore_signal(barrier, inc=1, device_id=(gx + dx, gy + dy, sa), device_id_type=MESH)
    for d in range(1, SA):
        pl.semaphore_signal(barrier, inc=1, device_id=(gx, gy, peers[d]), device_id_type=MESH)

    load = pltpu.make_async_copy(vals_hbm, vals, local_sem)
    load.start()

    shot = lax.broadcasted_iota(jnp.int32, (N, BLK), 0)
    gains = jnp.zeros((N, BLK), jnp.float32)
    for s in range(N):
        gains = jnp.where(shot == s, gain[group[s]], gains)
    for pair in range(NS // 2):
        halves = [source[:, (2 * pair + h) * BLK:(2 * pair + h + 1) * BLK].astype(jnp.float32) * gains for h in (0, 1)]
        scaled_all[sa, pair * 16:(pair + 1) * 16, :] = jnp.concatenate(halves, axis=0).astype(jnp.bfloat16)

    load.wait()
    pl.semaphore_wait(barrier, 3 + odd + sum(there.astype(jnp.int32) for there, _, _ in near))

    def copy(src, dst, send, recv, dx=0, dy=0, to=None):
        return pltpu.make_async_remote_copy(src, dst, send, recv, device_id=(gx + dx, gy + dy, sa if to is None else to),
                                            device_id_type=MESH)

    def scaled_copy(owner, peer):
        return copy(scaled_all.at[owner], scaled_all.at[owner], s_send.at[peer], s_recv.at[owner], to=peer)

    def part_copy(owner, peer):
        return copy(part_send.at[peer], part.at[owner], p_send.at[peer], p_recv.at[owner], to=peer)

    def weight_copy(k, owner, peer):
        rows = pl.ds(owner * OWN, OWN)
        return copy(vals.at[:, k:k + 1], weights.at[rows, k:k + 1], w_send.at[k, peer], w_recv.at[k, owner], to=peer)

    def own_copy(k, p):
        rows = pl.ds(p * OWN, OWN)
        return pltpu.make_async_copy(vals.at[:, k:k + 1], weights.at[rows, k:k + 1], w_recv.at[k, p])

    needed = (has_west, has_south)

    def send_weights():
        for k in (1, 0):
            @pl.when(needed[k])
            def _():
                for d in (2, 1, 3):
                    weight_copy(k, sa, peers[d]).start()

    def arrived(p):
        for k in (1, 0):
            @pl.when(needed[k])
            def _():
                own_copy(k, p).wait()

    def shuffle_copy(owner):
        lot = OWN - SENT
        return copy(vals.at[pl.ds(SENT, lot), 0:2], stage.at[pl.ds(owner * lot, lot)], h_send, h_recv.at[owner], to=SA - 1)

    def move_copy(k, h, last):
        rows = pl.ds(h * HALF, HALF)
        src = stage.at[rows, k] if last else vals.at[rows, k]
        return copy(src, moved.at[sa, k, rows], z_send.at[k, h], m_recv.at[k, h, sa], dx=-1)

    def moved_copy(k, h, owner, peer):
        ref = moved.at[owner, k, pl.ds(h * HALF, HALF)]
        return copy(ref, ref, m_send.at[k, h, peer], m_recv.at[k, h, owner], to=peer)

    part_move = copy(part_moved, part_m, z_more.at[0], e_recv.at[0], dx=-1)
    cols_move = copy(cols_hbm, cols_vmem, z_more.at[1], e_recv.at[1], dx=-1)

    def moves(act, chunks):
        for last in (False, True):
            @pl.when((sa == SA - 1) if last else (sa < SA - 1))
            def _():
                for k, h in chunks:
                    pl.when(needed[k])(lambda: act(move_copy(k, h, last)))

    def start_moves():
        moves(lambda c: c.start(), CHUNKS)

    early = donor & (jnp.logical_not(z_odd) | (z == 1))
    late = donor & z_odd & (z > 1)

    @pl.when(donor & (sa < SA - 1))
    def _():
        shuffle_copy(sa).start()
    pl.when(donor)(lambda: cols_move.start())
    pl.when(early & (sa < SA - 1))(start_moves)
    for d in (2, 1, 3):
        scaled_copy(sa, peers[d]).start()
    pl.when(ends)(lambda: pl.semaphore_signal(ack_sem, inc=1, device_id=(gx - 1, gy, sa), device_id_type=MESH))

    @pl.when(donor & (sa == SA - 1))
    def _():
        for owner in range(SA - 1):
            shuffle_copy(owner).wait_recv()
        pl.when(early)(start_moves)

    for d in (1, 3, 2):
        scaled_copy(peers[d], peers[d]).wait_recv()
    for p in range(SA):
        for pair in range(NS // 2):
            both = scaled_all[p, pair * 16:(pair + 1) * 16, :].astype(jnp.float32)
            picked_src[2 * pair, p * N:(p + 1) * N, :] = both[:N]
            picked_src[2 * pair + 1, p * N:(p + 1) * N, :] = both[N:]
    for r in range(OWN):
        o = sa * OWN + r
        left = jnp.concatenate([picked_src[cols[2, o]], picked_src[cols[3, o]]], axis=1).astype(jnp.bfloat16)
        out = jnp.dot(left, vals[r, 2:4].reshape(2 * BLK, BLK), preferred_element_type=jnp.float32)
        for p in range(SA):
            part_send[p, r] = out[p * N:(p + 1) * N]
    for d in (2, 1, 3):
        part_copy(sa, peers[d]).start()

    pl.when(works & (sa < SA - 1))(send_weights)
    gathers = works | (sa == SA - 1)
    for k in (1, 0):
        @pl.when(needed[k] & gathers)
        def _():
            own_copy(k, sa).start()

        @pl.when(jnp.logical_not(needed[k]))
        def _():
            weights[:, k] = jnp.zeros((OUTB, BLK, BLK), jnp.bfloat16)
    part[sa] = part_send[sa]
    for d in (1, 3, 2):
        part_copy(peers[d], peers[d]).wait_recv()

    def unpack(ref, dst, base):
        for pair in range(NT // 2):
            both = ref[pair * 16:(pair + 1) * 16, :].astype(jnp.float32)
            dst[base + 2 * pair] = both[:N]
            dst[base + 2 * pair + 1] = both[N:]

    def clear(dst, base):
        for b in range(NT):
            dst[base + b] = jnp.zeros((N, BLK), jnp.float32)

    def row(o):
        left = jnp.concatenate([traces[cols[0, o]], traces[cols[1, o]]], axis=1).astype(jnp.bfloat16)
        out = jnp.dot(left, weights[o].reshape(2 * BLK, BLK), preferred_element_type=jnp.float32)
        return out + part[o // OWN, o % OWN]

    def row_m(o):
        left = jnp.concatenate([traces_m[cols_m[0, o]], traces_m[cols_m[1, o]]], axis=1).astype(jnp.bfloat16)
        p, r = sent_slot(o)
        blocks = jnp.concatenate([moved[p, 0, r], moved[p, 1, r]], axis=0)
        return jnp.dot(left, blocks, preferred_element_type=jnp.float32)

    def interior():
        for o in range(TRACED, OUTB):
            inner_out[:, (o - TRACED) * BLK:(o - TRACED + 1) * BLK] = row(o).astype(jnp.bfloat16)

    def put_out():
        for ref, out in ((east, east_out), (north, north_out)):
            for pair in range(NT // 2):
                both = ref[pair * 16:(pair + 1) * 16, :]
                out[:, 2 * pair * BLK:(2 * pair + 1) * BLK] = both[:N]
                out[:, (2 * pair + 1) * BLK:(2 * pair + 2) * BLK] = both[N:]

    west_copy = copy(east_m, west, t_send.at[0], t_recv.at[0], dx=2)
    west_end_copy = copy(east, west, t_send.at[0], t_recv.at[0], dx=1)
    south_copy = copy(north, south, t_send.at[1], t_recv.at[1], dy=1)
    south_m_copy = copy(north_m, south_m, t_send.at[2], t_recv.at[2], dy=1)
    back_west = copy(east, west, t_send.at[3], t_recv.at[0], dx=1)
    back_south = copy(south_m, south, t_send.at[4], t_recv.at[1], dx=1)
    back_east = copy(east_m, east, t_send.at[5], t_recv.at[3], dx=1)
    back_north = copy(north_m, north, t_send.at[6], t_recv.at[4], dx=1)

    @pl.when(donor)
    def _():
        for o in range(0, TRACED, 2):
            both = jnp.concatenate([part[o // OWN, o % OWN], part[o // OWN, o % OWN + 1]], axis=0)
            part_moved[o * N:(o + 2) * N, :] = both.astype(jnp.bfloat16)

        @pl.when(late)
        def _():
            pl.semaphore_wait(go_sem, 1)
            start_moves()
        part_move.start()
        moves(lambda c: c.wait_send(), CHUNKS)
        part_move.wait_send()

        @pl.when(chains)
        def _():
            pl.semaphore_signal(go_sem, inc=1, device_id=(gx, gy + 4, sa), device_id_type=MESH)
        pl.when(sa == SA - 1)(send_weights)
        arrived(SA - 1)
        back_west.wait_recv()
        unpack(west, traces, NS)

        @pl.when(has_south)
        def _():
            back_south.wait_recv()
            unpack(south, traces, NS + NT)
        pl.when(jnp.logical_not(has_south))(lambda: clear(traces, NS + NT))
        interior()
        back_east.wait_recv()
        back_north.wait_recv()
        put_out()
        cols_move.wait_send()
        pl.when(sa < SA - 1)(lambda: shuffle_copy(sa).wait_send())

        @pl.when(sa == SA - 1)
        def _():
            for k in (0, 1):
                @pl.when(needed[k])
                def _():
                    for d in (1, 2, 3):
                        weight_copy(k, sa, peers[d]).wait_send()

    @pl.when(works)
    def _():
        for p in range(SA - 1):
            arrived(p)

    needed_m = (gx >= 0, has_south)

    def do_native():
        @pl.when(has_south)
        def _():
            south_copy.wait_recv()
            unpack(south, traces, NS + NT)
        pl.when(jnp.logical_not(has_south))(lambda: clear(traces, NS + NT))
        @pl.when(has_west)
        def _():
            west_copy.wait_recv()
            unpack(west, traces, NS)
        pl.when(jnp.logical_not(has_west))(lambda: clear(traces, NS))
        for base, ref in ((NT, north), (0, east)):
            for o in range(base, base + NT, 2):
                both = jnp.concatenate([row(o), row(o + 1)], axis=0)
                ref[(o - base) * N:(o - base + 2) * N, :] = both.astype(jnp.bfloat16)
            if base:
                pl.when(has_north)(lambda: south_copy.start())

        @pl.when(before_end)
        def _():
            pl.semaphore_wait(ack_sem, 1)
            west_end_copy.start()

    @pl.when(host)
    def _():
        @pl.when(jnp.logical_not(has_south))
        def _():
            for p in range(SA):
                moved[p, 1] = jnp.zeros((SENT, BLK, BLK), jnp.bfloat16)
        for k, h in CHUNKS:
            @pl.when(needed_m[k])
            def _():
                moved_copy(k, h, sa, peers[1]).wait_recv()
                for d in (2, 1, 3):
                    moved_copy(k, h, sa, peers[d]).start()
        cols_move.wait_recv()
        to_smem = pltpu.make_async_copy(cols_vmem, cols_m, local_sem)
        to_smem.start()
        to_smem.wait()
        part_move.wait_recv()
        for k, h in CHUNKS:
            @pl.when(needed_m[k])
            def _():
                for d in (1, 3, 2):
                    moved_copy(k, h, peers[d], sa).wait_recv()

    pl.when(works & (sa == SA - 1))(send_weights)
    pl.when(works)(do_native)

    @pl.when(host)
    def _():
        unpack(east, traces_m, NS)

        @pl.when(has_south)
        def _():
            south_m_copy.wait_recv()
            unpack(south_m, traces_m, NS + NT)
        pl.when(jnp.logical_not(has_south))(lambda: clear(traces_m, NS + NT))
        for base, ref in ((NT, north_m), (0, east_m)):
            for o in range(base, base + NT, 2):
                both = jnp.concatenate([row_m(o), row_m(o + 1)], axis=0)
                both = (both + part_m[o * N:(o + 2) * N, :].astype(jnp.float32)).astype(jnp.bfloat16)
                ref[(o - base) * N:(o - base + 2) * N, :] = both
            if base:
                pl.when(has_north)(lambda: south_m_copy.start())
        west_copy.start()
        back_west.start()
        pl.when(has_south)(lambda: back_south.start())
        back_east.start()
        back_north.start()

    @pl.when(works)
    def _():
        arrived(SA - 1)
        interior()
        put_out()
        for d in (1, 2, 3):
            for k in (0, 1):
                @pl.when(needed[k])
                def _():
                    weight_copy(k, sa, peers[d]).wait_send()
        pl.when(has_north)(lambda: south_copy.wait_send())
        pl.when(before_end)(lambda: west_end_copy.wait_send())

        @pl.when(host)
        def _():
            for k, h in CHUNKS:
                @pl.when(needed_m[k])
                def _():
                    for d in (1, 2, 3):
                        moved_copy(k, h, sa, peers[d]).wait_send()
            pl.when(has_north)(lambda: south_m_copy.wait_send())
            west_copy.wait_send()
            back_west.wait_send()
            pl.when(has_south)(lambda: back_south.wait_send())
            back_east.wait_send()
            back_north.wait_send()

    for d in (1, 2, 3):
        scaled_copy(sa, peers[d]).wait_send()
        part_copy(sa, peers[d]).wait_send()


def on_device(nx, ny, source, group_gain, shot_group, block_cols, block_vals):
    vmem, smem, hbm = (pl.BlockSpec(memory_space=m) for m in (pltpu.VMEM, pltpu.SMEM, pl.ANY))
    dma = pltpu.SemaphoreType.DMA
    bf16, f32 = jnp.bfloat16, jnp.float32
    trace = pltpu.VMEM((NT * N, BLK), bf16)
    cols = block_cols[0, 0].T
    outs = pl.pallas_call(
        functools.partial(kernel, nx, ny),
        out_shape=[jax.ShapeDtypeStruct((N, NT * BLK), bf16), jax.ShapeDtypeStruct((N, NT * BLK), bf16),
                   jax.ShapeDtypeStruct((N, (OUTB - TRACED) * BLK), bf16)],
        in_specs=[vmem, smem, smem, smem, hbm, hbm],
        out_specs=[vmem, vmem, vmem],
        scratch_shapes=[
            pltpu.VMEM((OUTB, 2, BLK, BLK), bf16),
            pltpu.VMEM((OWN, 4, BLK, BLK), bf16),
            pltpu.VMEM((SA, NS * N, BLK), bf16),
            pltpu.VMEM((NS, SA * N, BLK), f32),
            pltpu.VMEM((SA, OWN, N, BLK), f32),
            pltpu.VMEM((SA, OWN, N, BLK), f32),
            pltpu.VMEM((NS + 2 * NT, N, BLK), f32),
            trace, trace, trace, trace,
            pltpu.VMEM((SA, 2, SENT, BLK, BLK), bf16),
            pltpu.VMEM((SENT, 2, BLK, BLK), bf16),
            pltpu.VMEM((TRACED * N, BLK), bf16),
            pltpu.VMEM((TRACED * N, BLK), bf16),
            pltpu.VMEM(cols.shape, jnp.int32),
            pltpu.SMEM(cols.shape, jnp.int32),
            pltpu.VMEM((NS + 2 * NT, N, BLK), f32),
            trace, trace, trace,
            dma, dma((2, SA)), dma((2, SA)), dma((SA,)), dma((SA,)), dma((SA,)), dma((SA,)), dma((7,)), dma((5,)),
            dma, dma((SA - 1,)), dma((2, 2)), dma((2,)), dma((2,)), dma((2, 2, SA)), dma((2, 2, SA)),
            pltpu.SemaphoreType.REGULAR, pltpu.SemaphoreType.REGULAR,
        ],
        compiler_params=pltpu.CompilerParams(collective_id=0, has_side_effects=True, vmem_limit_bytes=63 << 20),
        name="sweep",
    )(source[0, 0], group_gain, shot_group, cols, cols, block_vals[0, 0])
    return tuple(out[None, None] for out in outs)


def solution(mesh):
    placed = (
        P("gx", "gy", "sa", None),
        P(),
        P("sa"),
        P("gx", "gy", None, None),
        P("gx", "gy", "sa", None, None, None),
    )
    return jax.shard_map(
        functools.partial(on_device, mesh.shape["gx"], mesh.shape["gy"]),
        mesh=mesh,
        in_specs=placed,
        out_specs=(P("gx", "gy", "sa", None), P("gx", "gy", "sa", None), P("gx", "gy", "sa", None)),
        check_vma=False,
    )
```

time: 102 us -> 100 us (0.980)
  the two profiles are of different devices: /device:TPU:255 before, /device:TPU:511 now
where the time goes in v4:
time: 100 us; the launch traced here: 99.7 us
  Pallas kernels  96.4 us (96%)
  local copies, waits for them, and re-layouts  2.69 us (3%)
    pallas_call x1, Pallas kernels, on_device(): pl.pallas_call(functools.partial(kernel, nx, ny), out_shape=[jax.ShapeDty...  96.4 us
    unnamed x7, local copies, waits for them, and re-layouts  2.69 us

profile of v4, /device:TPU:511, one launch (start us, length us, event | category | flops | bytes accessed | tf_op | source)
XLA Modules:
  0.0 99.7 jit_solution(4393101915892519502)
XLA Ops:
  0.6 96.4 %sweep.1 = (bf16[8,1536]{1,0:T(8,128)(2,1)}, bf16[8,1536]{1,0:T(8,128)(2,1)}, bf16[8,1024]{1,0:T(8,128)(2,1)}) custom-call(bf16[8,768]{1,0:T(8,128)(2,1)} %bitcast.12, f32[4]{0:T(128)} %gain.1, s32[8]{0:T(128)} %group.1, s32[4,32]{1,0:T(4,128)} %bitcast.13, s32[4,32]{1,0:T(4,128)} %bitcast.14, bf16[8,4,128,128]{3,2,1,0:T(8,128)(2,1)} %bitcast.8), custom_call_target="tpu_custom_call" | custom-call | tf_op jit(solution)/shard_map/sweep/pallas_call | solution.py:382
  97.0 0.0 copy-start
  97.0 1.4 %copy.11 = bf16[1,1,8,1536]{3,2,1,0:T(8,128)(2,1)} copy(bf16[1,1,8,1536]{3,2,1,0:T(8,128)(2,1)} %bitcast.10) | data formatting | bytes 49152
  98.4 0.0 copy-done
  98.4 0.0 copy-start.1
  98.4 0.6 copy.12
  99.0 0.1 copy-done.1
  99.1 0.6 copy.13
Async XLA Ops:
  97.0 1.4 %copy-start = (bf16[8,1536]{1,0:T(8,128)(2,1)S(1)}, bf16[8,1536]{1,0:T(8,128)(2,1)}, u32[]{:S(2)}) copy-start(bf16[8,1536]{1,0:T(8,128)(2,1)} %get-tuple-element.7) | copy-start | bytes 73732
  98.4 0.7 copy-start.1

commit v5 on v4

--- a/solution.py
+++ b/solution.py
@@ -16,23 +16,34 @@
 OWN = OUTB // SA
 N = 8
 TRACED = 2 * NT
-SENT = TRACED // SA
-
-HALF = SENT // 2
 CHUNKS = ((0, 0), (0, 1), (1, 0), (1, 1))
-
-
-def sent_slot(o):
+SENT = (6, 7)
+LOT = tuple(OWN - sent for sent in SENT)
+
+
+def piece(k, h, last):
+    count = (SA - 1) * LOT[k] if last else SENT[k]
+    first = (count + 1) // 2
+    return pl.ds(first, count - first) if h else pl.ds(0, first)
+
+
+def sent_slot(o, k):
     owner, r = divmod(o, OWN)
-    return (owner, r) if r < SENT else (SA - 1, (OWN - SENT) * owner + r - SENT)
+    return (owner, r) if r < SENT[k] else (SA - 1, LOT[k] * owner + r - SENT[k])
+
+
+def each(owner, act):
+    pl.when(owner < SA - 1)(lambda: act(False))
+    pl.when(owner == SA - 1)(lambda: act(True))
 
 
 def kernel(nx, ny, source, gain, group, cols, cols_hbm, vals_hbm, east_out, north_out, inner_out,
            weights, vals, scaled_all, picked_src, part_send, part, traces, west, south, east, north,
-           moved, stage, part_moved, part_m, cols_vmem, cols_m, traces_m, south_m, east_m, north_m,
+           moved_w, moved_s, stage_w, stage_s, part_moved, part_m, cols_vmem, cols_m, traces_m, south_m, east_m, north_m,
            local_sem, w_send, w_recv, s_send, s_recv, p_send, p_recv, t_send, t_recv,
-           h_send, h_recv, z_send, z_more, e_recv, m_send, m_recv, go_sem, ack_sem):
+           h_send, h_recv, z_send, z_more, e_recv, m_send, m_recv, f_send, f_moved, go_sem, ack_sem):
     gx, gy, sa = lax.axis_index("gx"), lax.axis_index("gy"), lax.axis_index("sa")
+    moved, stage = (moved_w, moved_s), (stage_w, stage_s)
     odd = lax.rem(gx, 2)
     z = gy // 2
     peers = [lax.rem(sa + d, SA) for d in range(SA)]
@@ -93,12 +104,15 @@
 
     needed = (has_west, has_south)
 
-    def send_weights():
+    def weights_do(act, ds):
         for k in (1, 0):
             @pl.when(needed[k])
             def _():
-                for d in (2, 1, 3):
-                    weight_copy(k, sa, peers[d]).start()
+                for d in ds:
+                    act(weight_copy(k, sa, peers[d]))
+
+    def send_interior():
+        weights_do(lambda c: c.start(), (2, 1, 3))
 
     def arrived(p):
         for k in (1, 0):
@@ -106,17 +120,27 @@
             def _():
                 own_copy(k, p).wait()
 
-    def shuffle_copy(owner):
-        lot = OWN - SENT
-        return copy(vals.at[pl.ds(SENT, lot), 0:2], stage.at[pl.ds(owner * lot, lot)], h_send, h_recv.at[owner], to=SA - 1)
+    def pass_on(k, d):
+        rows = pl.ds(peers[d] * OWN, OWN)
+        ref = weights.at[rows, k:k + 1]
+        return copy(ref, ref, f_send.at[k], w_recv.at[k, peers[d]], to=peers[SA - d])
+
+    def pass_moved(k, h, last):
+        d = 1 if h else SA - 1
+        ref = moved[k].at[peers[d], piece(k, h, last)]
+        return copy(ref, ref, f_moved.at[k, h], m_recv.at[k, h, peers[d]], to=peers[SA - d])
+
+    def shuffle_copy(k, owner):
+        return copy(vals.at[pl.ds(SENT[k], LOT[k]), k], stage[k].at[pl.ds(owner * LOT[k], LOT[k])], h_send.at[k],
+                    h_recv.at[k, owner], to=SA - 1)
 
     def move_copy(k, h, last):
-        rows = pl.ds(h * HALF, HALF)
-        src = stage.at[rows, k] if last else vals.at[rows, k]
-        return copy(src, moved.at[sa, k, rows], z_send.at[k, h], m_recv.at[k, h, sa], dx=-1)
-
-    def moved_copy(k, h, owner, peer):
-        ref = moved.at[owner, k, pl.ds(h * HALF, HALF)]
+        rows = piece(k, h, last)
+        src = stage[k].at[rows] if last else vals.at[rows, k]
+        return copy(src, moved[k].at[sa, rows], z_send.at[k, h], m_recv.at[k, h, sa], dx=-1)
+
+    def moved_copy(k, h, owner, peer, last):
+        ref = moved[k].at[owner, piece(k, h, last)]
         return copy(ref, ref, m_send.at[k, h, peer], m_recv.at[k, h, owner], to=peer)
 
     part_move = copy(part_moved, part_m, z_more.at[0], e_recv.at[0], dx=-1)
@@ -137,7 +161,8 @@
 
     @pl.when(donor & (sa < SA - 1))
     def _():
-        shuffle_copy(sa).start()
+        for k in (0, 1):
+            shuffle_copy(k, sa).start()
     pl.when(donor)(lambda: cols_move.start())
     pl.when(early & (sa < SA - 1))(start_moves)
     for d in (2, 1, 3):
@@ -147,7 +172,8 @@
     @pl.when(donor & (sa == SA - 1))
     def _():
         for owner in range(SA - 1):
-            shuffle_copy(owner).wait_recv()
+            for k in (0, 1):
+                shuffle_copy(k, owner).wait_recv()
         pl.when(early)(start_moves)
 
     for d in (1, 3, 2):
@@ -166,7 +192,7 @@
     for d in (2, 1, 3):
         part_copy(sa, peers[d]).start()
 
-    pl.when(works & (sa < SA - 1))(send_weights)
+    pl.when(works & (sa < SA - 1))(lambda: weights_do(lambda c: c.start(), (1, 3)))
     gathers = works | (sa == SA - 1)
     for k in (1, 0):
         @pl.when(needed[k] & gathers)
@@ -197,8 +223,7 @@
 
     def row_m(o):
         left = jnp.concatenate([traces_m[cols_m[0, o]], traces_m[cols_m[1, o]]], axis=1).astype(jnp.bfloat16)
-        p, r = sent_slot(o)
-        blocks = jnp.concatenate([moved[p, 0, r], moved[p, 1, r]], axis=0)
+        blocks = jnp.concatenate([moved[k][sent_slot(o, k)] for k in (0, 1)], axis=0)
         return jnp.dot(left, blocks, preferred_element_type=jnp.float32)
 
     def interior():
@@ -238,7 +263,7 @@
         @pl.when(chains)
         def _():
             pl.semaphore_signal(go_sem, inc=1, device_id=(gx, gy + 4, sa), device_id_type=MESH)
-        pl.when(sa == SA - 1)(send_weights)
+        pl.when(sa == SA - 1)(send_interior)
         arrived(SA - 1)
         back_west.wait_recv()
         unpack(west, traces, NS)
@@ -253,20 +278,27 @@
         back_north.wait_recv()
         put_out()
         cols_move.wait_send()
-        pl.when(sa < SA - 1)(lambda: shuffle_copy(sa).wait_send())
-
-        @pl.when(sa == SA - 1)
-        def _():
-            for k in (0, 1):
-                @pl.when(needed[k])
-                def _():
-                    for d in (1, 2, 3):
-                        weight_copy(k, sa, peers[d]).wait_send()
+        for k in (0, 1):
+            pl.when(sa < SA - 1)(lambda: shuffle_copy(k, sa).wait_send())
+
+        pl.when(sa == SA - 1)(lambda: weights_do(lambda c: c.wait_send(), (1, 2, 3)))
+
+    passes = ((1, 1), (0, 3))
 
     @pl.when(works)
     def _():
-        for p in range(SA - 1):
-            arrived(p)
+        for k, d in passes:
+            @pl.when(needed[k] & (peers[d] < SA - 1))
+            def _():
+                own_copy(k, peers[d]).wait()
+                pass_on(k, d).start()
+        for d in range(SA):
+            for k in (1, 0):
+                if (k, d) not in passes:
+                    @pl.when(needed[k] & (peers[d] < SA - 1))
+                    def _():
+                        own_copy(k, peers[d]).wait()
+        pl.when((sa == SA - 1) & ((gx >= nx - 2) | (z >= 4)))(send_interior)
 
     needed_m = (gx >= 0, has_south)
 
@@ -298,13 +330,22 @@
         @pl.when(jnp.logical_not(has_south))
         def _():
             for p in range(SA):
-                moved[p, 1] = jnp.zeros((SENT, BLK, BLK), jnp.bfloat16)
+                moved[1][p] = jnp.zeros((SENT[1], BLK, BLK), jnp.bfloat16)
         for k, h in CHUNKS:
             @pl.when(needed_m[k])
             def _():
-                moved_copy(k, h, sa, peers[1]).wait_recv()
-                for d in (2, 1, 3):
-                    moved_copy(k, h, sa, peers[d]).start()
+                def move_on(last):
+                    moved_copy(k, h, sa, peers[1], last).wait_recv()
+                    for d in (1, 3):
+                        moved_copy(k, h, sa, peers[d], last).start()
+                each(sa, move_on)
+        for k, h in CHUNKS:
+            @pl.when(needed_m[k])
+            def _():
+                def move_on(last):
+                    moved_copy(k, h, peers[1 if h else SA - 1], sa, last).wait_recv()
+                    pass_moved(k, h, last).start()
+                each(peers[1 if h else SA - 1], move_on)
         cols_move.wait_recv()
         to_smem = pltpu.make_async_copy(cols_vmem, cols_m, local_sem)
         to_smem.start()
@@ -313,10 +354,9 @@
         for k, h in CHUNKS:
             @pl.when(needed_m[k])
             def _():
-                for d in (1, 3, 2):
-                    moved_copy(k, h, peers[d], sa).wait_recv()
-
-    pl.when(works & (sa == SA - 1))(send_weights)
+                for d in (SA - 1 if h else 1, 2):
+                    each(peers[d], lambda last: moved_copy(k, h, peers[d], sa, last).wait_recv())
+
     pl.when(works)(do_native)
 
     @pl.when(host)
@@ -340,17 +380,17 @@
         pl.when(has_south)(lambda: back_south.start())
         back_east.start()
         back_north.start()
+        pl.when((sa == SA - 1) & (z < 4))(send_interior)
 
     @pl.when(works)
     def _():
         arrived(SA - 1)
         interior()
         put_out()
-        for d in (1, 2, 3):
-            for k in (0, 1):
-                @pl.when(needed[k])
-                def _():
-                    weight_copy(k, sa, peers[d]).wait_send()
+        pl.when(sa < SA - 1)(lambda: weights_do(lambda c: c.wait_send(), (1, 3)))
+        pl.when(sa == SA - 1)(lambda: weights_do(lambda c: c.wait_send(), (1, 2, 3)))
+        for k, d in passes:
+            pl.when(needed[k] & (peers[d] < SA - 1))(lambda: pass_on(k, d).wait_send())
         pl.when(has_north)(lambda: south_copy.wait_send())
         pl.when(before_end)(lambda: west_end_copy.wait_send())
 
@@ -359,8 +399,9 @@
             for k, h in CHUNKS:
                 @pl.when(needed_m[k])
                 def _():
-                    for d in (1, 2, 3):
-                        moved_copy(k, h, sa, peers[d]).wait_send()
+                    for d in (1, 3):
+                        each(sa, lambda last: moved_copy(k, h, sa, peers[d], last).wait_send())
+                    each(peers[1 if h else SA - 1], lambda last: pass_moved(k, h, last).wait_send())
             pl.when(has_north)(lambda: south_m_copy.wait_send())
             west_copy.wait_send()
             back_west.wait_send()
@@ -394,8 +435,8 @@
             pltpu.VMEM((SA, OWN, N, BLK), f32),
             pltpu.VMEM((NS + 2 * NT, N, BLK), f32),
             trace, trace, trace, trace,
-            pltpu.VMEM((SA, 2, SENT, BLK, BLK), bf16),
-            pltpu.VMEM((SENT, 2, BLK, BLK), bf16),
+            *[pltpu.VMEM((SA, sent, BLK, BLK), bf16) for sent in SENT],
+            *[pltpu.VMEM(((SA - 1) * lot, BLK, BLK), bf16) for lot in LOT],
             pltpu.VMEM((TRACED * N, BLK), bf16),
             pltpu.VMEM((TRACED * N, BLK), bf16),
             pltpu.VMEM(cols.shape, jnp.int32),
@@ -403,7 +444,7 @@
             pltpu.VMEM((NS + 2 * NT, N, BLK), f32),
             trace, trace, trace,
             dma, dma((2, SA)), dma((2, SA)), dma((SA,)), dma((SA,)), dma((SA,)), dma((SA,)), dma((7,)), dma((5,)),
-            dma, dma((SA - 1,)), dma((2, 2)), dma((2,)), dma((2,)), dma((2, 2, SA)), dma((2, 2, SA)),
+            dma((2,)), dma((2, SA - 1)), dma((2, 2)), dma((2,)), dma((2,)), dma((2, 2, SA)), dma((2, 2, SA)), dma((2,)), dma((2, 2)),
             pltpu.SemaphoreType.REGULAR, pltpu.SemaphoreType.REGULAR,
         ],
         compiler_params=pltpu.CompilerParams(collective_id=0, has_side_effects=True, vmem_limit_bytes=63 << 20),

time: 100 us -> 96.3 us (0.963)
  the two profiles are of different devices: /device:TPU:511 before, /device:TPU:505 now
where the time goes in v5:
time: 96.3 us; the launch traced here: 96 us
  Pallas kernels  92.7 us (96%)
  local copies, waits for them, and re-layouts  2.69 us (3%)
    pallas_call x1, Pallas kernels, on_device(): pl.pallas_call(functools.partial(kernel, nx, ny), out_shape=[jax.ShapeDty...  92.7 us
    unnamed x7, local copies, waits for them, and re-layouts  2.69 us

profile of v5, /device:TPU:505, one launch (start us, length us, event | category | flops | bytes accessed | tf_op | source)
XLA Modules:
  0.0 96.0 jit_solution(4635043731098039354)
XLA Ops:
  0.6 92.7 %sweep.1 = (bf16[8,1536]{1,0:T(8,128)(2,1)}, bf16[8,1536]{1,0:T(8,128)(2,1)}, bf16[8,1024]{1,0:T(8,128)(2,1)}) custom-call(bf16[8,768]{1,0:T(8,128)(2,1)} %bitcast.12, f32[4]{0:T(128)} %gain.1, s32[8]{0:T(128)} %group.1, s32[4,32]{1,0:T(4,128)} %bitcast.13, s32[4,32]{1,0:T(4,128)} %bitcast.14, bf16[8,4,128,128]{3,2,1,0:T(8,128)(2,1)} %bitcast.8), custom_call_target="tpu_custom_call" | custom-call | tf_op jit(solution)/shard_map/sweep/pallas_call | solution.py:423
  93.3 0.0 copy-start
  93.3 1.4 %copy.11 = bf16[1,1,8,1536]{3,2,1,0:T(8,128)(2,1)} copy(bf16[1,1,8,1536]{3,2,1,0:T(8,128)(2,1)} %bitcast.10) | data formatting | bytes 49152
  94.7 0.0 copy-done
  94.7 0.0 copy-start.1
  94.7 0.6 copy.12
  95.3 0.1 copy-done.1
  95.4 0.6 copy.13
Async XLA Ops:
  93.3 1.4 %copy-start = (bf16[8,1536]{1,0:T(8,128)(2,1)S(1)}, bf16[8,1536]{1,0:T(8,128)(2,1)}, u32[]{:S(2)}) copy-start(bf16[8,1536]{1,0:T(8,128)(2,1)} %get-tuple-element.7) | copy-start | bytes 73732
  94.7 0.7 copy-start.1

commit v6 on v5

--- a/solution.py
+++ b/solution.py
@@ -19,6 +19,9 @@
 CHUNKS = ((0, 0), (0, 1), (1, 0), (1, 1))
 SENT = (6, 7)
 LOT = tuple(OWN - sent for sent in SENT)
+
+
+STEP = 2
 
 
 def piece(k, h, last):
@@ -153,8 +156,23 @@
                 for k, h in chunks:
                     pl.when(needed[k])(lambda: act(move_copy(k, h, last)))
 
+    gated = jnp.logical_not(z_odd) & (z >= 4)
+
     def start_moves():
-        moves(lambda c: c.start(), CHUNKS)
+        pl.when(jnp.logical_not(gated))(lambda: moves(lambda c: c.start(), CHUNKS))
+
+        @pl.when(gated)
+        def _():
+            for k, h in CHUNKS:
+                def bit_by_bit(last):
+                    src = stage[k] if last else vals.at[:, k]
+                    rows = piece(k, h, last)
+                    for r in range(rows.start, rows.start + rows.size, STEP):
+                        some = pl.ds(r, min(STEP, rows.start + rows.size - r))
+                        c = copy(src.at[some], moved[k].at[sa, some], z_send.at[k, h], m_recv.at[k, h, sa], dx=-1)
+                        c.start()
+                        c.wait_send()
+                pl.when(needed[k])(lambda: each(sa, bit_by_bit))
 
     early = donor & (jnp.logical_not(z_odd) | (z == 1))
     late = donor & z_odd & (z > 1)
@@ -257,7 +275,7 @@
             pl.semaphore_wait(go_sem, 1)
             start_moves()
         part_move.start()
-        moves(lambda c: c.wait_send(), CHUNKS)
+        pl.when(jnp.logical_not(gated))(lambda: moves(lambda c: c.wait_send(), CHUNKS))
         part_move.wait_send()
 
         @pl.when(chains)
@@ -447,7 +465,7 @@
             dma((2,)), dma((2, SA - 1)), dma((2, 2)), dma((2,)), dma((2,)), dma((2, 2, SA)), dma((2, 2, SA)), dma((2,)), dma((2, 2)),
             pltpu.SemaphoreType.REGULAR, pltpu.SemaphoreType.REGULAR,
         ],
-        compiler_params=pltpu.CompilerParams(collective_id=0, has_side_effects=True, vmem_limit_bytes=63 << 20),
+        compiler_params=pltpu.CompilerParams(collective_id=0, has_side_effects=True, vmem_limit_bytes=107 << 19),
         name="sweep",
     )(source[0, 0], group_gain, shot_group, cols, cols, block_vals[0, 0])
     return tuple(out[None, None] for out in outs)

time: 96.3 us -> 93.6 us (0.972)
  Pallas kernels: 92.7 us -> 89.5 us
    pallas_call x1, Pallas kernels: 92.7 us -> 89.5 us  [on_device(): pl.pallas_call(functools.partial(kernel, nx, ny), out_shape=[jax.ShapeDty...]
    unnamed x7 -> x11, local copies, waits for them, and re-layouts: 2.69 us -> 3.19 us
where the time goes in v6:
time: 93.6 us; the launch traced here: 93.3 us
  Pallas kernels  89.5 us (96%)
  local copies, waits for them, and re-layouts  3.19 us (3%)
    pallas_call x1, Pallas kernels, on_device(): pl.pallas_call(functools.partial(kernel, nx, ny), out_shape=[jax.ShapeDty...  89.5 us
    unnamed x11, local copies, waits for them, and re-layouts  3.19 us

profile of v6, /device:TPU:505, one launch (start us, length us, event | category | flops | bytes accessed | tf_op | source)
XLA Modules:
  0.0 93.3 jit_solution(6531333254880882222)
XLA Ops:
  0.6 0.0 copy-start.1
  0.6 0.0 copy-start.2
  0.7 0.0 copy-start.3
  0.7 0.7 copy-done.1
  1.3 0.0 copy-done.2
  1.3 0.0 copy-done.3
  1.3 0.0 copy-start
  1.3 0.7 copy-done
  2.0 89.5 %sweep.1 = (bf16[8,1536]{1,0:T(8,128)(2,1)S(1)}, bf16[8,1536]{1,0:T(8,128)(2,1)S(1)}, bf16[8,1024]{1,0:T(8,128)(2,1)S(1)}) custom-call(bf16[8,768]{1,0:T(8,128)(2,1)S(1)} %bitcast.11, f32[4]{0:T(128)S(1)} %copy-done.2, s32[8]{0:T(128)S(1)} %copy-done.3, s32[4,32]{1,0:T(4,128)S(1)} %bitcast.12, s32[4,32]{1,0:T(4,128)S(1)} %bitcast.13, ...), custom_call_target="tpu_custom_call" | custom-call | tf_op jit(solution)/shard_map/sweep/pallas_call | solution.py:441
  91.5 0.6 copy.11
  92.1 0.6 copy.12
  92.7 0.6 copy.13
Async XLA Ops:
  0.6 0.7 copy-start.1
  0.6 0.7 copy-start.2
  0.7 0.7 copy-start.3
  1.3 0.7 copy-start

commit v7 on v6

--- a/solution.py
+++ b/solution.py
@@ -156,7 +156,7 @@
                 for k, h in chunks:
                     pl.when(needed[k])(lambda: act(move_copy(k, h, last)))
 
-    gated = jnp.logical_not(z_odd) & (z >= 4)
+    gated = jnp.logical_not(z_odd) & (z >= 2)
 
     def start_moves():
         pl.when(jnp.logical_not(gated))(lambda: moves(lambda c: c.start(), CHUNKS))
@@ -316,7 +316,7 @@
                     @pl.when(needed[k] & (peers[d] < SA - 1))
                     def _():
                         own_copy(k, peers[d]).wait()
-        pl.when((sa == SA - 1) & ((gx >= nx - 2) | (z >= 4)))(send_interior)
+        pl.when((sa == SA - 1) & ((gx >= nx - 2) | (z >= 5)))(send_interior)
 
     needed_m = (gx >= 0, has_south)
 
@@ -398,7 +398,7 @@
         pl.when(has_south)(lambda: back_south.start())
         back_east.start()
         back_north.start()
-        pl.when((sa == SA - 1) & (z < 4))(send_interior)
+        pl.when((sa == SA - 1) & (z < 5))(send_interior)
 
     @pl.when(works)
     def _():

time: 93.6 us -> 93.7 us (level)
  no operation moved by 1% of the time
where the time goes in v7:
time: 93.7 us; the launch traced here: 93.5 us
  Pallas kernels  89.6 us (96%)
  local copies, waits for them, and re-layouts  3.19 us (3%)
    pallas_call x1, Pallas kernels, on_device(): pl.pallas_call(functools.partial(kernel, nx, ny), out_shape=[jax.ShapeDty...  89.6 us
    unnamed x11, local copies, waits for them, and re-layouts  3.19 us

profile of v7, /device:TPU:505, one launch (start us, length us, event | category | flops | bytes accessed | tf_op | source)
XLA Modules:
  0.0 93.5 jit_solution(12929392090469194350)
XLA Ops:
  0.6 0.0 copy-start.1
  0.6 0.0 copy-start.2
  0.7 0.0 copy-start.3
  0.7 0.7 copy-done.1
  1.3 0.0 copy-done.2
  1.3 0.0 copy-done.3
  1.3 0.0 copy-start
  1.3 0.7 copy-done
  2.0 89.6 %sweep.1 = (bf16[8,1536]{1,0:T(8,128)(2,1)S(1)}, bf16[8,1536]{1,0:T(8,128)(2,1)S(1)}, bf16[8,1024]{1,0:T(8,128)(2,1)S(1)}) custom-call(bf16[8,768]{1,0:T(8,128)(2,1)S(1)} %bitcast.11, f32[4]{0:T(128)S(1)} %copy-done.2, s32[8]{0:T(128)S(1)} %copy-done.3, s32[4,32]{1,0:T(4,128)S(1)} %bitcast.12, s32[4,32]{1,0:T(4,128)S(1)} %bitcast.13, ...), custom_call_target="tpu_custom_call" | custom-call | tf_op jit(solution)/shard_map/sweep/pallas_call | solution.py:441
  91.6 0.6 copy.11
  92.3 0.6 copy.12
  92.9 0.6 copy.13
Async XLA Ops:
  0.6 0.7 copy-start.1
  0.6 0.7 copy-start.2
  0.7 0.7 copy-start.3
  1.3 0.7 copy-start

commit v8 on v6

--- a/solution.py
+++ b/solution.py
@@ -276,11 +276,11 @@
             start_moves()
         part_move.start()
         pl.when(jnp.logical_not(gated))(lambda: moves(lambda c: c.wait_send(), CHUNKS))
+
+        @pl.when(chains)
+        def _():
+            pl.semaphore_signal(go_sem, inc=1, device_id=(gx, gy + 4, sa), device_id_type=MESH)
         part_move.wait_send()
-
-        @pl.when(chains)
-        def _():
-            pl.semaphore_signal(go_sem, inc=1, device_id=(gx, gy + 4, sa), device_id_type=MESH)
         pl.when(sa == SA - 1)(send_interior)
         arrived(SA - 1)
         back_west.wait_recv()

time: 93.6 us -> 93.6 us (level)
  no operation moved by 1% of the time
where the time goes in v8:
time: 93.6 us; the launch traced here: 93.3 us
  Pallas kernels  89.5 us (96%)
  local copies, waits for them, and re-layouts  3.19 us (3%)
    pallas_call x1, Pallas kernels, on_device(): pl.pallas_call(functools.partial(kernel, nx, ny), out_shape=[jax.ShapeDty...  89.5 us
    unnamed x11, local copies, waits for them, and re-layouts  3.19 us

profile of v8, /device:TPU:505, one launch (start us, length us, event | category | flops | bytes accessed | tf_op | source)
XLA Modules:
  0.0 93.3 jit_solution(6025122239196145915)
XLA Ops:
  0.6 0.0 copy-start.1
  0.6 0.0 copy-start.2
  0.7 0.0 copy-start.3
  0.7 0.7 copy-done.1
  1.3 0.0 copy-done.2
  1.3 0.0 copy-done.3
  1.3 0.0 copy-start
  1.3 0.7 copy-done
  2.0 89.5 %sweep.1 = (bf16[8,1536]{1,0:T(8,128)(2,1)S(1)}, bf16[8,1536]{1,0:T(8,128)(2,1)S(1)}, bf16[8,1024]{1,0:T(8,128)(2,1)S(1)}) custom-call(bf16[8,768]{1,0:T(8,128)(2,1)S(1)} %bitcast.11, f32[4]{0:T(128)S(1)} %copy-done.2, s32[8]{0:T(128)S(1)} %copy-done.3, s32[4,32]{1,0:T(4,128)S(1)} %bitcast.12, s32[4,32]{1,0:T(4,128)S(1)} %bitcast.13, ...), custom_call_target="tpu_custom_call" | custom-call | tf_op jit(solution)/shard_map/sweep/pallas_call | solution.py:441
  91.5 0.6 copy.11
  92.1 0.6 copy.12
  92.7 0.6 copy.13
Async XLA Ops:
  0.6 0.7 copy-start.1
  0.6 0.7 copy-start.2
  0.7 0.7 copy-start.3
  1.3 0.7 copy-start
